TPU v7x, 512 devices: a whole 4x4x16 slice. The times are simulated.
512 devices in a mesh: clip: 8 (over y, x_hi), tok: 64 (over x_lo, z, core).
Axes of the slice: x: 4 (x_hi: 2, x_lo: 2; x = x_hi * 2 + x_lo), y: 4, z: 16, core: 2. Of those that a mesh axis runs over, the one named last changes fastest.
Arguments:
- student_hidden: bfloat16 [8, 16384, 1024], P('clip', 'tok'), may hold values from -120 to 120
- teacher_tokens: bfloat16 [8, 16384, 1024], P('clip', 'tok'), may hold values from -120 to 120
- proj_weight: bfloat16 [1024, 1024], replicated, may hold values from -0.1875 to 0.1875
Outputs:
- hidden_grad: bfloat16 [8, 16384, 1024], P('clip', 'tok')
- weight_grad: float32 [1024, 1024], P('tok')
All inputs are finite; a program needn't handle non-finite values.
Results may differ from a plain program's by a relative error of at most 0.012.
Values may be sent and summed in bfloat16 or wider, within the bound.
A program may use at most 64 MiB of HBM per device.

v0:
```python
import jax
import jax.numpy as jnp
from jax import lax
from jax.sharding import PartitionSpec as P

BAND = 4


EPSILON = 1e-06


def passed_along(array, axis, by):
    length = lax.axis_size(axis)
    pairs = [(i, i + by) for i in range(length) if 0 <= i + by < length]
    return lax.ppermute(array, axis, pairs)


def inner_rows(first, second):
    return lax.dot_general(
        first, second, (((1,), (1,)), ((), ())), preferred_element_type=jnp.float32
    )


def inner_cols(first, second):
    return lax.dot_general(
        first, second, (((0,), (0,)), ((), ())), preferred_element_type=jnp.float32
    )


def unit_rows(values):
    row_norm = jnp.sqrt(jnp.sum(values * values, axis=-1, keepdims=True) + EPSILON)
    return (values / row_norm, row_norm)


def pair_weight(own_student, own_teacher, far_student, far_teacher):
    pair_diff = inner_rows(own_student, far_student) - inner_rows(own_teacher, far_teacher)
    return (256.0 * pair_diff).astype(jnp.bfloat16)


def local(student_hidden, teacher_tokens, proj_weight):
    hidden = student_hidden[0]
    teacher = teacher_tokens[0]
    tok_rows = hidden.shape[0]
    projected = jnp.dot(hidden, proj_weight, preferred_element_type=jnp.float32)
    unit, row_norm = unit_rows(projected)
    own_student = unit.astype(jnp.bfloat16)
    own_teacher = unit_rows(teacher.astype(jnp.float32))[0].astype(jnp.bfloat16)
    own_diff = inner_rows(own_student, own_student) - inner_rows(own_teacher, own_teacher)
    own_weight = (128.0 * (own_diff + own_diff.T)).astype(jnp.bfloat16)
    unit_grad = jnp.dot(own_weight, own_student, preferred_element_type=jnp.float32)
    for distance in range(1, BAND + 1):
        far_student, far_teacher = passed_along((own_student, own_teacher), "tok", -distance)
        weights = pair_weight(own_student, own_teacher, far_student, far_teacher)
        unit_grad = unit_grad + jnp.dot(weights, far_student, preferred_element_type=jnp.float32)
        returned = inner_cols(weights, own_student)
        unit_grad = unit_grad + passed_along(returned.astype(jnp.bfloat16), "tok", distance).astype(
            returned.dtype
        )
    along = jnp.sum(unit * unit_grad, axis=-1, keepdims=True)
    proj_grad = ((unit_grad - unit * along) / row_norm).astype(jnp.bfloat16)
    hidden_grad = inner_rows(proj_grad, proj_weight).astype(jnp.bfloat16)
    grad_scale = 1.0 / (4.0 * tok_rows)
    share_grad = lax.psum_scatter(
        inner_cols(hidden, proj_grad) * grad_scale, "tok", scatter_dimension=0, tiled=True
    )
    weight_grad = lax.psum(share_grad.astype(jnp.bfloat16), "clip").astype(jnp.float32)
    return (hidden_grad[None], weight_grad)


def solution(mesh):
    placed = (P("clip", "tok", None), P("clip", "tok", None), P())
    return jax.shard_map(
        local,
        mesh=mesh,
        in_specs=placed,
        out_specs=(P("clip", "tok", None), P("tok", None)),
        check_vma=False,
    )
```

profile of v0, /device:TPU:2, one launch (start us, length us, event | category | flops | bytes accessed | tf_op | source)
XLA Modules:
  0.0 475.8 jit_solution(5189615401115343340)
XLA Ops:
  7.2 0.0 copy-start
  7.2 0.0 reduce-scatter.4.cloned.1.call-start
  7.2 1.4 fusion.18
  8.6 1.3 fusion.19
  9.9 11.8 %collective-permute-start.10 = (bf16[256,1024]{1,0:T(8,128)(2,1)S(1)}, bf16[256,1024]{1,0:T(8,128)(2,1)}, u32[]{:S(2)}, u32[]{:S(2)}) collective-permute-start(bf16[256,1024]{1,0:T(8,128)(2,1)S(1)} %fusion.19), channel_id=1, source_target_pairs={{4,0},{5,1},{6,2},{7,3},{8,4},{9,5},{10,6},{11,7},{12,8},{13,9},{1... | collective-permute-start | bytes 1572872 | tf_op jit(solution)/shard_map/ppermute | solution.py:15
  21.7 2.5 collective-permute-start.7
  24.2 4.1 collective-permute-start.4
  28.4 2.8 collective-permute-start.1
  31.1 0.0 copy-done
  31.1 1.8 multiply_reduce_fusion.1
  33.0 0.0 copy-start.3
  33.0 0.9 copy-done.1
  33.9 0.1 fusion.33
  34.1 3.4 collective-permute-start.9
  37.5 0.3 fusion.34
  37.8 0.0 copy-done.3
  37.8 0.4 convolution_subtract_fusion.4
  38.3 0.8 copy.7
  39.1 1.2 fusion.29
  40.3 5.5 %collective-permute-done.10 = bf16[256,1024]{1,0:T(8,128)(2,1)} collective-permute-done((bf16[256,1024]{1,0:T(8,128)(2,1)S(1)}, bf16[256,1024]{1,0:T(8,128)(2,1)}, u32[]{:S(2)}, u32[]{:S(2)}) %collective-permute-start.10) | collective-permute-done | bytes 524320 | tf_op jit(solution)/shard_map/ppermute | solution.py:15
  45.9 6.4 %collective-permute-start.6 = (bf16[256,1024]{1,0:T(8,128)(2,1)S(1)}, bf16[256,1024]{1,0:T(8,128)(2,1)S(1)}, u32[]{:S(2)}, u32[]{:S(2)}) collective-permute-start(bf16[256,1024]{1,0:T(8,128)(2,1)S(1)} %fusion.33), channel_id=1, source_target_pairs={{3,0},{4,1},{5,2},{6,3},{7,4},{8,5},{9,6},{10,7},{11,8},{12,9},{13... | collective-permute-start | bytes 1572872 | tf_op jit(solution)/shard_map/ppermute | solution.py:15
  52.3 1.4 fusion.40
  53.7 8.4 %collective-permute-done.7 = bf16[256,1024]{1,0:T(8,128)(2,1)} collective-permute-done((bf16[256,1024]{1,0:T(8,128)(2,1)S(1)}, bf16[256,1024]{1,0:T(8,128)(2,1)}, u32[]{:S(2)}, u32[]{:S(2)}) %collective-permute-start.7) | collective-permute-done | bytes 524320 | tf_op jit(solution)/shard_map/ppermute | solution.py:15
  62.0 4.4 collective-permute-start.3
  66.5 1.4 fusion.38
  67.8 39.8 %collective-permute-done.9 = bf16[256,1024]{1,0:T(8,128)(2,1)} collective-permute-done((bf16[256,1024]{1,0:T(8,128)(2,1)S(1)}, bf16[256,1024]{1,0:T(8,128)(2,1)}, u32[]{:S(2)}, u32[]{:S(2)}) %collective-permute-start.9) | collective-permute-done | bytes 524320 | tf_op jit(solution)/shard_map/ppermute | solution.py:15
  107.7 1.9 collective-permute-start
  109.6 1.4 fusion.14
  111.0 0.3 convolution_convert_fusion
  111.3 11.4 %collective-permute-done.6 = bf16[256,1024]{1,0:T(8,128)(2,1)S(1)} collective-permute-done((bf16[256,1024]{1,0:T(8,128)(2,1)S(1)}, bf16[256,1024]{1,0:T(8,128)(2,1)S(1)}, u32[]{:S(2)}, u32[]{:S(2)}) %collective-permute-start.6) | collective-permute-done | bytes 524320 | tf_op jit(solution)/shard_map/ppermute | solution.py:15
  122.7 1.9 collective-permute-start.11
  124.7 0.3 fusion.15
  125.0 0.3 convolution_convert_fusion.1
  125.3 0.0 collective-permute-done.4
  125.3 1.9 collective-permute-start.8
  127.3 1.4 fusion.36
  128.7 0.0 collective-permute-done.3
  128.7 0.3 fusion.16
  129.0 0.3 convolution_convert_fusion.2
  129.3 3.5 collective-permute-start.5
  132.8 0.0 collective-permute-done.1
  132.9 1.4 fusion.35
  134.2 0.0 collective-permute-done
  134.3 0.3 fusion.17
  134.6 0.3 convolution_convert_fusion.3
  134.9 1.9 collective-permute-start.2
  136.9 1.3 fusion.41
  138.2 0.3 fusion.39
  138.5 0.3 fusion.37
  138.8 13.7 %collective-permute-done.11 = bf16[256,1024]{1,0:T(8,128)(2,1)S(1)} collective-permute-done((bf16[256,1024]{1,0:T(8,128)(2,1)S(1)}, bf16[256,1024]{1,0:T(8,128)(2,1)S(1)}, u32[]{:S(2)}, u32[]{:S(2)}) %collective-permute-start.11) | collective-permute-done | bytes 524320 | tf_op jit(solution)/shard_map/ppermute | solution.py:15
  152.5 15.6 %collective-permute-done.8 = bf16[256,1024]{1,0:T(8,128)(2,1)S(1)} collective-permute-done((bf16[256,1024]{1,0:T(8,128)(2,1)S(1)}, bf16[256,1024]{1,0:T(8,128)(2,1)S(1)}, u32[]{:S(2)}, u32[]{:S(2)}) %collective-permute-start.8) | collective-permute-done | bytes 524320 | tf_op jit(solution)/shard_map/ppermute | solution.py:15
  168.1 9.9 %collective-permute-done.5 = bf16[256,1024]{1,0:T(8,128)(2,1)S(1)} collective-permute-done((bf16[256,1024]{1,0:T(8,128)(2,1)S(1)}, bf16[256,1024]{1,0:T(8,128)(2,1)S(1)}, u32[]{:S(2)}, u32[]{:S(2)}) %collective-permute-start.5) | collective-permute-done | bytes 524320 | tf_op jit(solution)/shard_map/ppermute | solution.py:15
  178.1 5.3 %collective-permute-done.2 = bf16[256,1024]{1,0:T(8,128)(2,1)S(1)} collective-permute-done((bf16[256,1024]{1,0:T(8,128)(2,1)S(1)}, bf16[256,1024]{1,0:T(8,128)(2,1)S(1)}, u32[]{:S(2)}, u32[]{:S(2)}) %collective-permute-start.2) | collective-permute-done | bytes 524320 | tf_op jit(solution)/shard_map/ppermute | solution.py:15
  183.4 0.8 multiply_reduce_fusion
  184.2 0.2 divide_convert_fusion
  184.4 0.8 copy-done.4
  185.2 2.8 multiply_bitcast_fusion
  188.0 5.4 %copy.9 = f32[1024,1024]{1,0:T(8,128)} copy(f32[1024,1024]{0,1:T(8,128)} %multiply_bitcast_fusion) | data formatting | bytes 8388608
  193.4 0.0 reduce-scatter.4.cloned.1.call-update
  193.4 1.5 fusion.9
  194.9 226.9 %reduce-scatter.4.cloned.1.call-done = f32[16,1024]{1,0:T(8,128)} async-done(((f32[1024,1024]{1,0:T(8,128)}), f32[16,1024]{1,0:T(8,128)}) %reduce-scatter.4.cloned.1.call-update) | async-done | bytes 65552
  421.8 1.0 copy.10
  422.8 45.5 %psum.7 = bf16[16,1024]{0,1:T(8,128)(2,1)S(1)} all-reduce(bf16[16,1024]{0,1:T(8,128)(2,1)S(1)} %copy.10), channel_id=1, replica_groups=mesh['clip'=8,'tok'=64] {'clip'}, use_global_device_ids=true, to_apply=%region_4.0 | all-reduce | flops 16384 | bytes 65536 | tf_op jit(solution)/shard_map/psum | solution.py:66
  468.3 0.7 copy.8
  (6 shorter events, 0.0 us)
Async XLA Ops:
  7.2 24.0 %copy-start = (bf16[1024,1024]{1,0:T(8,128)(2,1)S(1)}, bf16[1024,1024]{1,0:T(8,128)(2,1)}, u32[]{:S(2)}) copy-start(bf16[1024,1024]{1,0:T(8,128)(2,1)} %param.5) | copy-start | bytes 6291460
  7.2 414.6 %reduce-scatter.4.cloned.1.call-start = ((), (), s32[]{:S(2)}) async-start(), calls=%async_computation.1 | async-start | bytes 4259840
  9.9 36.0 %collective-permute-start.10 = (bf16[256,1024]{1,0:T(8,128)(2,1)S(1)}, bf16[256,1024]{1,0:T(8,128)(2,1)}, u32[]{:S(2)}, u32[]{:S(2)}) collective-permute-start(bf16[256,1024]{1,0:T(8,128)(2,1)S(1)} %fusion.19), channel_id=1, source_target_pairs={{4,0},{5,1},{6,2},{7,3},{8,4},{9,5},{10,6},{11,7},{12,8},{13,9},{1... | collective-permute-start | bytes 1572872 | tf_op jit(solution)/shard_map/ppermute | solution.py:15
  21.7 40.3 %collective-permute-start.7 = (bf16[256,1024]{1,0:T(8,128)(2,1)S(1)}, bf16[256,1024]{1,0:T(8,128)(2,1)}, u32[]{:S(2)}, u32[]{:S(2)}) collective-permute-start(bf16[256,1024]{1,0:T(8,128)(2,1)S(1)} %fusion.19), channel_id=1, source_target_pairs={{3,0},{4,1},{5,2},{6,3},{7,4},{8,5},{9,6},{10,7},{11,8},{12,9},{13... | collective-permute-start | bytes 1572872 | tf_op jit(solution)/shard_map/ppermute | solution.py:15
  24.2 101.1 %collective-permute-start.4 = (bf16[256,1024]{1,0:T(8,128)(2,1)S(1)}, bf16[256,1024]{1,0:T(8,128)(2,1)}, u32[]{:S(2)}, u32[]{:S(2)}) collective-permute-start(bf16[256,1024]{1,0:T(8,128)(2,1)S(1)} %fusion.19), channel_id=1, source_target_pairs={{2,0},{3,1},{4,2},{5,3},{6,4},{7,5},{8,6},{9,7},{10,8},{11,9},{12,... | collective-permute-start | bytes 1572872 | tf_op jit(solution)/shard_map/ppermute | solution.py:15
  28.4 104.5 %collective-permute-start.1 = (bf16[256,1024]{1,0:T(8,128)(2,1)S(1)}, bf16[256,1024]{1,0:T(8,128)(2,1)}, u32[]{:S(2)}, u32[]{:S(2)}) collective-permute-start(bf16[256,1024]{1,0:T(8,128)(2,1)S(1)} %fusion.19), channel_id=1, source_target_pairs={{1,0},{2,1},{3,2},{4,3},{5,4},{6,5},{7,6},{8,7},{9,8},{10,9},{11,1... | collective-permute-start | bytes 1572872 | tf_op jit(solution)/shard_map/ppermute | solution.py:15
  33.0 1.0 copy-start.1
  33.0 4.8 %copy-start.3 = (bf16[1,256,1024]{2,1,0:T(8,128)(2,1)S(1)}, bf16[1,256,1024]{2,1,0:T(8,128)(2,1)}, u32[]{:S(2)}) copy-start(bf16[1,256,1024]{2,1,0:T(8,128)(2,1)} %param.4) | copy-start | bytes 1572868
  34.1 73.6 %collective-permute-start.9 = (bf16[256,1024]{1,0:T(8,128)(2,1)S(1)}, bf16[256,1024]{1,0:T(8,128)(2,1)}, u32[]{:S(2)}, u32[]{:S(2)}) collective-permute-start(bf16[256,1024]{1,0:T(8,128)(2,1)S(1)} %fusion.33), channel_id=1, source_target_pairs={{4,0},{5,1},{6,2},{7,3},{8,4},{9,5},{10,6},{11,7},{12,8},{13,9},{1... | collective-permute-start | bytes 1572872 | tf_op jit(solution)/shard_map/ppermute | solution.py:15
  45.9 76.8 %collective-permute-start.6 = (bf16[256,1024]{1,0:T(8,128)(2,1)S(1)}, bf16[256,1024]{1,0:T(8,128)(2,1)S(1)}, u32[]{:S(2)}, u32[]{:S(2)}) collective-permute-start(bf16[256,1024]{1,0:T(8,128)(2,1)S(1)} %fusion.33), channel_id=1, source_target_pairs={{3,0},{4,1},{5,2},{6,3},{7,4},{8,5},{9,6},{10,7},{11,8},{12,9},{13... | collective-permute-start | bytes 1572872 | tf_op jit(solution)/shard_map/ppermute | solution.py:15
  62.0 66.6 %collective-permute-start.3 = (bf16[256,1024]{1,0:T(8,128)(2,1)S(1)}, bf16[256,1024]{1,0:T(8,128)(2,1)S(1)}, u32[]{:S(2)}, u32[]{:S(2)}) collective-permute-start(bf16[256,1024]{1,0:T(8,128)(2,1)S(1)} %fusion.33), channel_id=1, source_target_pairs={{2,0},{3,1},{4,2},{5,3},{6,4},{7,5},{8,6},{9,7},{10,8},{11,9},{12,... | collective-permute-start | bytes 1572872 | tf_op jit(solution)/shard_map/ppermute | solution.py:15
  107.7 26.6 %collective-permute-start = (bf16[256,1024]{1,0:T(8,128)(2,1)S(1)}, bf16[256,1024]{1,0:T(8,128)(2,1)S(1)}, u32[]{:S(2)}, u32[]{:S(2)}) collective-permute-start(bf16[256,1024]{1,0:T(8,128)(2,1)S(1)} %fusion.33), channel_id=1, source_target_pairs={{1,0},{2,1},{3,2},{4,3},{5,4},{6,5},{7,6},{8,7},{9,8},{10,9},{11,1... | collective-permute-start | bytes 1572872 | tf_op jit(solution)/shard_map/ppermute | solution.py:15
  122.7 29.8 %collective-permute-start.11 = (bf16[256,1024]{1,0:T(8,128)(2,1)S(1)}, bf16[256,1024]{1,0:T(8,128)(2,1)S(1)}, u32[]{:S(2)}, u32[]{:S(2)}) collective-permute-start(bf16[256,1024]{1,0:T(8,128)(2,1)S(1)} %convolution_convert_fusion), channel_id=1, source_target_pairs={{0,4},{1,5},{2,6},{3,7},{4,8},{5,9},{6,10},{7,11},{8,12},{9,13},{1... | collective-permute-start | bytes 1572872 | tf_op jit(solution)/shard_map/ppermute | solution.py:15
  125.3 42.8 %collective-permute-start.8 = (bf16[256,1024]{1,0:T(8,128)(2,1)S(1)}, bf16[256,1024]{1,0:T(8,128)(2,1)S(1)}, u32[]{:S(2)}, u32[]{:S(2)}) collective-permute-start(bf16[256,1024]{1,0:T(8,128)(2,1)S(1)} %convolution_convert_fusion.1), channel_id=1, source_target_pairs={{0,3},{1,4},{2,5},{3,6},{4,7},{5,8},{6,9},{7,10},{8,11},{9,12},{10... | collective-permute-start | bytes 1572872 | tf_op jit(solution)/shard_map/ppermute | solution.py:15
  129.3 48.7 %collective-permute-start.5 = (bf16[256,1024]{1,0:T(8,128)(2,1)S(1)}, bf16[256,1024]{1,0:T(8,128)(2,1)S(1)}, u32[]{:S(2)}, u32[]{:S(2)}) collective-permute-start(bf16[256,1024]{1,0:T(8,128)(2,1)S(1)} %convolution_convert_fusion.2), channel_id=1, source_target_pairs={{0,2},{1,3},{2,4},{3,5},{4,6},{5,7},{6,8},{7,9},{8,10},{9,11},{10,... | collective-permute-start | bytes 1572872 | tf_op jit(solution)/shard_map/ppermute | solution.py:15
  134.9 48.5 %collective-permute-start.2 = (bf16[256,1024]{1,0:T(8,128)(2,1)S(1)}, bf16[256,1024]{1,0:T(8,128)(2,1)S(1)}, u32[]{:S(2)}, u32[]{:S(2)}) collective-permute-start(bf16[256,1024]{1,0:T(8,128)(2,1)S(1)} %convolution_convert_fusion.3), channel_id=1, source_target_pairs={{0,1},{1,2},{2,3},{3,4},{4,5},{5,6},{6,7},{7,8},{8,9},{9,10},{10,1... | collective-permute-start | bytes 1572872 | tf_op jit(solution)/shard_map/ppermute | solution.py:15
  138.2 45.2 %copy-start.2 = (f32[256,1024]{1,0:T(8,128)S(1)}, f32[256,1024]{1,0:T(8,128)}, u32[]{:S(2)}) copy-start(f32[256,1024]{1,0:T(8,128)} %copy-done.1) | copy-start | bytes 3145732
  184.2 1.0 copy-start.4
Sparse Core Ops, SparseCore 0:
  193.5 228.2 reduce-scatter.3
where the time goes:
time: 477 us; the launch traced here: 476 us
  waiting for transfers between devices  337 us (71%)
  starting transfers between devices  46.6 us (10%)
  blocking collectives  45.5 us (10%)
  matrix products  20.1 us (4%)
  between operations  14.4 us (3%)
  local copies, waits for them, and re-layouts  9.7 us (2%)
    unnamed x2, waiting for transfers between devices  227 us
    ppermute x12, waiting for transfers between devices, passed_along(): return lax.ppermute(array, axis, pairs)  110 us
    ppermute x12, starting transfers between devices, passed_along(): return lax.ppermute(array, axis, pairs)  46.5 us
    psum x1, blocking collectives, local(): lax.psum(share_grad.astype(jnp.bfloat16), 'clip').astype(jnp.float32)  45.5 us
    dot_general x11, matrix products, inner_rows(): lax.dot_general(first, second, (((1,), (1,)), ((), ())), preferred_elemen...  10.2 us
  transfers between devices with their start and end apart: 13, of which 9 were waited for; matrix products, arithmetic and copies ran while one was open for 4% of the time, Pallas kernels for 0%

commit v1 on v0

v1 whole, which is shorter than its diff:
```python
import jax
import jax.numpy as jnp
from jax import lax
from jax.experimental import pallas as pl
from jax.experimental.pallas import tpu as pltpu
from jax.sharding import PartitionSpec as P

EPSILON = 1e-06
MESH = pl.DeviceIdType.MESH
BF16 = jnp.bfloat16
F32 = jnp.float32
ROWS = 256
FEAT = 1024
NZ, NY, NX, NCLIP = 16, 4, 4, 8
CHAINS = 32
HALF = 2
STEP = 32


def dot_nn(a, b):
    return jnp.dot(a, b, preferred_element_type=F32)


def dot_nt(a, b):
    return lax.dot_general(a, b, (((1,), (1,)), ((), ())), preferred_element_type=F32)


def kernel(
    h_ref, t_ref, w_ref, hg_ref, wg_ref,
    wv, hr, tr, su, tu, proj, inv, dt, e_near, e_far, g, pall, ht,
    ws, wr, a0, a1, r0, r1, b0, b1, s0, s1, zs, zr, ag, pf, hgv, ov,
    load_sem, store_sem, halo_s, halo_r, fwd_s, fwd_r, pf_s, pf_r,
    d2d_s, d2d_r, st1_s, st1_r, st1b_s, st1b_r, st2_s, st2_r, z_s, z_r, ag_s, ag_r,
):
    k = lax.axis_index("clip")
    b = lax.axis_index("tok")
    c = lax.rem(b, 2)
    q = b // 2
    z = lax.rem(q, NZ)
    xl = q // NZ
    y = k // 2
    xh = lax.rem(k, 2)
    x = xh * 2 + xl
    has = (q > 0, q < CHAINS - 1)

    def at(yy, xx, zz, cc):
        return {"clip": yy * 2 + xx // 2, "tok": lax.rem(xx, 2) * 32 + zz * 2 + cc}

    sib = {"clip": k, "tok": b + 1 - 2 * c}
    side = ({"clip": k, "tok": b - 2}, {"clip": k, "tok": b + 2})

    def y_peer(d):
        return at(lax.rem(y + d, NY), x, z, c)

    def x_peer(d):
        return at(y, lax.rem(x + d, NX), z, c)

    def z_peer(d):
        return at(y, x, lax.rem(z + d, NZ), c)

    def clip_peer(d):
        return {"clip": lax.rem(k + d, NCLIP), "tok": b}

    def remote(src, dst, ssem, rsem, dev):
        return pltpu.make_async_remote_copy(
            src_ref=src, dst_ref=dst, send_sem=ssem, recv_sem=rsem, device_id=dev, device_id_type=MESH
        )

    loads = [
        pltpu.make_async_copy(t_ref, tr.at[1], load_sem.at[0]),
        pltpu.make_async_copy(h_ref, hr.at[1], load_sem.at[1]),
        pltpu.make_async_copy(w_ref, wv, load_sem.at[2]),
    ]
    for cp in loads:
        cp.start()
    barrier = pltpu.get_barrier_semaphore()

    def greet(dev):
        pl.semaphore_signal(barrier, inc=1, device_id=dev, device_id_type=MESH)

    greet(sib)
    for i in range(2):
        @pl.when(has[i])
        def _(i=i):
            greet(side[i])
    greet(x_peer(1))
    greet(x_peer(3))
    for d in range(1, NCLIP):
        greet(clip_peer(d))
    for d in range(1, NZ):
        greet(z_peer(d))
    ends = jnp.where(q > 0, 1, 0) + jnp.where(q < CHAINS - 1, 1, 0)
    pl.semaphore_wait(barrier, 3 + (NCLIP - 1) + (NZ - 1) + ends)
    for cp in loads[:2]:
        cp.wait()

    hrows = ROWS // HALF

    def halo_copies(i):
        dst_slot = 2 - 2 * i
        copies = [remote(tr.at[1], tr.at[dst_slot], halo_s.at[i, 0], halo_r.at[i, 0], side[i])]
        for j in range(HALF):
            rows = pl.ds(j * hrows, hrows)
            copies.append(
                remote(
                    hr.at[1, rows], hr.at[dst_slot, rows], halo_s.at[i, 1 + j], halo_r.at[i, 1 + j], side[i]
                )
            )
        return copies

    halo = [halo_copies(0), halo_copies(1)]
    for n in range(1 + HALF):
        for i in range(2):
            @pl.when(has[i])
            def _(i=i, n=n):
                halo[i][n].start()

    def halo_arrival(slot, n):
        i = 0 if slot == 0 else 1
        src = halo[1 - i][n]

        @pl.when(has[i])
        def _():
            src.wait_recv()

        @pl.when(jnp.logical_not(has[i]))
        def _():
            if n == 0:
                tr[slot] = jnp.zeros((ROWS, FEAT), BF16)
            else:
                hr[slot, (n - 1) * hrows : n * hrows] = jnp.zeros((hrows, FEAT), BF16)

    def teacher_unit(slot):
        def body(i, carry):
            rows = pl.ds(pl.multiple_of(i * STEP, STEP), STEP)
            v = tr[slot, rows].astype(F32)
            r = lax.rsqrt(jnp.sum(v * v, axis=-1, keepdims=True) + EPSILON)
            tu[slot, 0, rows] = (v * r).astype(BF16)
            return carry

        lax.fori_loop(0, ROWS // STEP, body, 0)

    def student_unit(slot, r0_, n):
        rows_all = slice(r0_, r0_ + n)
        for nb in range(4):
            cols = slice(nb * 256, (nb + 1) * 256)
            proj[slot, rows_all, cols] = dot_nn(hr[slot, rows_all], wv[:, cols])

        def body(i, carry):
            rows = pl.ds(pl.multiple_of(r0_ + i * STEP, STEP), STEP)
            v = proj[slot, rows]
            r = lax.rsqrt(jnp.sum(v * v, axis=-1, keepdims=True) + EPSILON)
            inv[slot, rows] = jnp.broadcast_to(r, (STEP, 128))
            su[slot, 0, rows] = (v * r).astype(BF16)
            return carry

        lax.fori_loop(0, n // STEP, body, 0)

    def transposed(slot):
        for j in range(4):
            cols = slice(j * 256, (j + 1) * 256)
            v = hr[slot, :, cols].astype(F32).T.reshape(8, 2, 16, ROWS)
            for cc in range(2):
                ht[cc, j * 128 : (j + 1) * 128, slot * 256 : (slot + 1) * 256] = (
                    v[:, cc].reshape(128, ROWS).astype(BF16)
                )

    def forward(buf, slot, n):
        cp = remote(buf.at[slot, 0], buf.at[slot, 1], fwd_s.at[n, slot], fwd_r.at[n, slot], sib)
        cp.start()
        return cp

    fwd = {}
    teacher_unit(1)
    fwd["t1"] = forward(tu, 1, 0)
    loads[2].wait()
    student_unit(1, 0, ROWS)
    fwd["s1"] = forward(su, 1, 1)
    transposed(1)
    for slot in (0, 2):
        halo_arrival(slot, 0)
        teacher_unit(slot)
        fwd["t%d" % slot] = forward(tu, slot, 0)
    for slot in (1, 0, 2):
        fwd["t%d" % slot].wait_recv()

    def near_t(j, carry):
        dt[j] = dot_nt(tu[1, 0], tu[j // 2, lax.rem(j, 2)])
        return carry

    lax.fori_loop(0, 6, near_t, 0)
    for f in range(2):
        for who in range(2):
            dt[6 + f * 2 + who] = dot_nt(tu[2 * f, 0], tu[2 - 2 * f, who])

    for n in range(HALF):
        for slot in (0, 2):
            halo_arrival(slot, 1 + n)
            student_unit(slot, n * hrows, hrows)
            if n == HALF - 1:
                fwd["s%d" % slot] = forward(su, slot, 1)
    for slot in (0, 2):
        transposed(slot)
    for slot in (1, 0, 2):
        fwd["s%d" % slot].wait_recv()

    for j in range(6):
        e_near[:, j * 256 : (j + 1) * 256] = (
            256.0 * (dot_nt(su[1, 0], su[j // 2, j % 2]) - dt[j])
        ).astype(BF16)
    cross = (jnp.where(c == 1, 256.0, 0.0), jnp.where(c == 0, 256.0, 0.0))
    for f in range(2):
        for who in range(2):
            scale = 256.0 if who == 0 else cross[f]
            e_far[f, :, who * 256 : (who + 1) * 256] = (
                scale * (dot_nt(su[2 * f, 0], su[2 - 2 * f, who]) - dt[6 + f * 2 + who])
            ).astype(BF16)

    def stacked(lo, n, cols):
        return jnp.concatenate([su[(lo + i) // 2, (lo + i) % 2, :, cols] for i in range(n)], axis=0)

    for nb in range(4):
        cols = slice(nb * 256, (nb + 1) * 256)
        g[1, :, cols] = dot_nn(e_near[...], stacked(0, 6, cols))
        g[0, :, cols] = dot_nn(e_far[0], stacked(4, 2, cols))
        g[2, :, cols] = dot_nn(e_far[1], stacked(0, 2, cols))

    def project(slot):
        def body(i, carry):
            rows = pl.ds(pl.multiple_of(i * STEP, STEP), STEP)
            r = inv[slot, rows][:, :1]
            u = proj[slot, rows] * r
            v = g[slot, rows]
            along = jnp.sum(u * v, axis=-1, keepdims=True)
            out = pl.ds(pl.multiple_of(slot * ROWS + i * STEP, STEP), STEP)
            pall[out] = ((v - u * along) * r).astype(BF16)
            return carry

        lax.fori_loop(0, ROWS // STEP, body, 0)

    back = []
    for i, slot in ((0, 0), (1, 2)):
        project(slot)
        cp = remote(pall.at[pl.ds(slot * ROWS, ROWS)], pf.at[1 - i], pf_s.at[i], pf_r.at[i], side[i])
        back.append(cp)

        @pl.when(has[i])
        def _(cp=cp):
            cp.start()
    project(1)

    d2d = []
    for d in range(4):
        yy = lax.rem(y + 1 + d, NY)
        part = dot_nn(ht[1 - c], pall[:, pl.ds(pl.multiple_of(yy * 256, 256), 256)])
        for i in range(2):
            ws[d, i] = part[:, i * 128 : (i + 1) * 128].astype(BF16)
        cp = remote(ws.at[d], wr.at[d], d2d_s.at[d], d2d_r.at[d], sib)
        cp.start()
        d2d.append(cp)
    st1, st1b = [], []
    for d in range(4):
        dy = (1 + d) % 4
        yy = lax.rem(y + dy, NY)
        part = dot_nn(ht[c], pall[:, pl.ds(pl.multiple_of(yy * 256, 256), 256)])
        d2d[d].wait_recv()
        for i in range(2):
            v = (part[:, i * 128 : (i + 1) * 128] + wr[d, i].astype(F32)).astype(BF16)
            for j in range(2):
                a0[yy, i * 2 + j] = v[j * 256 : j * 256 + 128]
                a1[i * 2 + j, yy] = v[j * 256 + 128 : j * 256 + 256]
        if dy:
            cp = remote(a0.at[yy], r0.at[dy - 1], st1_s.at[dy - 1], st1_r.at[dy - 1], y_peer(dy))
            cp.start()
            st1.append(cp)
        for dx in range(1, NX):
            xx = lax.rem(x + dx, NX)
            cp = remote(
                a1.at[xx, yy], r1.at[dx - 1, yy], st1b_s.at[dx - 1, dy], st1b_r.at[dx - 1, dy], x_peer(dx)
            )
            cp.start()
            st1b.append(cp)

    st2 = []
    for cp in st1:
        cp.wait_recv()
    for dx in (1, 2, 3, 0):
        xx = lax.rem(x + dx, NX)
        v = a0[y, xx].astype(F32)
        for i in range(3):
            v = v + r0[i, xx].astype(F32)
        b0[xx] = v.astype(BF16)
        if dx:
            cp = remote(b0.at[xx], s0.at[dx - 1], st2_s.at[0, dx - 1], st2_r.at[0, dx - 1], x_peer(dx))
            cp.start()
            st2.append(cp)
    for cp in st1b:
        cp.wait_recv()
    for dy in (1, 2, 3, 0):
        yy = lax.rem(y + dy, NY)
        v = a1[x, yy].astype(F32)
        for i in range(3):
            v = v + r1[i, yy].astype(F32)
        b1[yy] = v.astype(BF16)
        if dy:
            cp = remote(b1.at[yy], s1.at[dy - 1], st2_s.at[1, dy - 1], st2_r.at[1, dy - 1], y_peer(dy))
            cp.start()
            st2.append(cp)
    for cp in st2:
        cp.wait_recv()
    v = b0[x].astype(F32)
    for i in range(3):
        v = v + s0[i].astype(F32)
    zs[0:8] = v.reshape(8, 16, 128).astype(BF16)
    v = b1[y].astype(F32)
    for i in range(3):
        v = v + s1[i].astype(F32)
    zs[8:16] = v.reshape(8, 16, 128).astype(BF16)
    zc = []
    for d in range(1, NZ):
        zz = lax.rem(z + d, NZ)
        cp = remote(zs.at[zz], zr.at[d - 1], z_s.at[d - 1], z_r.at[d - 1], z_peer(d))
        cp.start()
        zc.append(cp)

    for i in range(2):
        @pl.when(has[i])
        def _(i=i):
            back[1 - i].wait_recv()

        @pl.when(jnp.logical_not(has[i]))
        def _(i=i):
            pf[i] = jnp.zeros((ROWS, FEAT), BF16)

    def total(i, carry):
        rows = pl.ds(pl.multiple_of(i * STEP, STEP), STEP)
        own = pl.ds(pl.multiple_of(ROWS + i * STEP, STEP), STEP)
        v = pall[own].astype(F32) + pf[0, rows].astype(F32) + pf[1, rows].astype(F32)
        hgv[rows] = v.astype(BF16)
        return carry

    lax.fori_loop(0, ROWS // STEP, total, 0)
    ptot = hgv[...]
    for nb in range(4):
        cols = slice(nb * 256, (nb + 1) * 256)
        ov[:, cols] = dot_nt(ptot, wv[nb * 256 : (nb + 1) * 256]).astype(BF16)
    store = pltpu.make_async_copy(ov, hg_ref, store_sem.at[0])
    store.start()

    for cp in zc:
        cp.wait_recv()
    v = zs[z].astype(F32)
    for d in range(NZ - 1):
        v = v + zr[d].astype(F32)
    ag[k] = v * (1.0 / 1024.0)
    agc = []
    for d in range(1, NCLIP):
        cp = remote(ag.at[k], ag.at[k], ag_s.at[d - 1], ag_r.at[d - 1], clip_peer(d))
        cp.start()
        agc.append(cp)
    for cp in agc:
        cp.wait_recv()
    for i in range(NCLIP):
        wg_ref[:, i * 128 : (i + 1) * 128] = ag[i]

    for i in range(2):
        @pl.when(has[i])
        def _(i=i):
            for cp in halo[i]:
                cp.wait_send()
            back[i].wait_send()
    for cp in list(fwd.values()) + d2d + st1 + st1b + st2 + zc + agc:
        cp.wait_send()
    store.wait()


def local(student_hidden, teacher_tokens, proj_weight):
    dma = pltpu.SemaphoreType.DMA
    vm = pltpu.VMEM
    hidden_grad, weight_grad = pl.pallas_call(
        kernel,
        out_shape=(
            jax.ShapeDtypeStruct((ROWS, FEAT), BF16),
            jax.ShapeDtypeStruct((16, FEAT), F32),
        ),
        in_specs=[pl.BlockSpec(memory_space=pl.ANY)] * 3,
        out_specs=(pl.BlockSpec(memory_space=pl.ANY), pl.BlockSpec(memory_space=pltpu.VMEM)),
        scratch_shapes=[
            vm((FEAT, FEAT), BF16),
            vm((3, ROWS, FEAT), BF16),
            vm((3, ROWS, FEAT), BF16),
            vm((3, 2, ROWS, FEAT), BF16),
            vm((3, 2, ROWS, FEAT), BF16),
            vm((3, ROWS, FEAT), F32),
            vm((3, ROWS, 128), F32),
            vm((10, ROWS, ROWS), F32),
            vm((ROWS, 6 * ROWS), BF16),
            vm((2, ROWS, 2 * ROWS), BF16),
            vm((3, ROWS, FEAT), F32),
            vm((3 * ROWS, FEAT), BF16),
            vm((2, 512, 3 * ROWS), BF16),
            vm((4, 2, 512, 128), BF16),
            vm((4, 2, 512, 128), BF16),
            vm((4, 4, 128, 128), BF16),
            vm((4, 4, 128, 128), BF16),
            vm((3, 4, 128, 128), BF16),
            vm((3, 4, 128, 128), BF16),
            vm((4, 128, 128), BF16),
            vm((4, 128, 128), BF16),
            vm((3, 128, 128), BF16),
            vm((3, 128, 128), BF16),
            vm((NZ, 16, 128), BF16),
            vm((NZ - 1, 16, 128), BF16),
            vm((NCLIP, 16, 128), F32),
            vm((2, ROWS, FEAT), BF16),
            vm((ROWS, FEAT), BF16),
            vm((ROWS, FEAT), BF16),
            dma((3,)), dma((1,)),
            dma((2, 1 + HALF)), dma((2, 1 + HALF)),
            dma((2, 3)), dma((2, 3)),
            dma((2,)), dma((2,)),
            dma((4,)), dma((4,)),
            dma((3,)), dma((3,)),
            dma((3, 4)), dma((3, 4)),
            dma((2, 3)), dma((2, 3)),
            dma((NZ - 1,)), dma((NZ - 1,)),
            dma((NCLIP - 1,)), dma((NCLIP - 1,)),
        ],
        compiler_params=pltpu.CompilerParams(
            collective_id=0, has_side_effects=True, vmem_limit_bytes=56 * 2**20
        ),
    )(student_hidden[0], teacher_tokens[0], proj_weight)
    return hidden_grad[None], weight_grad


def solution(mesh):
    placed = (P("clip", "tok", None), P("clip", "tok", None), P())
    return jax.shard_map(
        local,
        mesh=mesh,
        in_specs=placed,
        out_specs=(P("clip", "tok", None), P("tok", None)),
        check_vma=False,
    )
```

time: 477 us -> 85.9 us (0.18)
  the two profiles are of different devices: /device:TPU:2 before, /device:TPU:32 now
where the time goes in v1:
time: 85.9 us; the launch traced here: 85.7 us
  Pallas kernels  81.7 us (95%)
  local copies, waits for them, and re-layouts  3.34 us (4%)
    pallas_call x1, Pallas kernels, local(): pl.pallas_call(kernel, out_shape=(jax.ShapeDtypeStruct((ROWS, FEAT), BF16...  81.7 us
    unnamed x2, local copies, waits for them, and re-layouts  3.34 us

profile of v1, /device:TPU:32, one launch (start us, length us, event | category | flops | bytes accessed | tf_op | source)
XLA Modules:
  0.0 85.7 jit_solution(17627014457118371201)
XLA Ops:
  0.6 81.7 %shard_map.50 = (bf16[256,1024]{1,0:T(8,128)(2,1)}, f32[16,1024]{1,0:T(8,128)}) custom-call(bf16[256,1024]{1,0:T(8,128)(2,1)} %bitcast.4, bf16[256,1024]{1,0:T(8,128)(2,1)} %bitcast.5, bf16[1024,1024]{1,0:T(8,128)(2,1)} %w_ref.1), custom_call_target="tpu_custom_call" | custom-call | tf_op jit(solution)/shard_map/pallas_call | solution.py:380
  82.4 1.9 %copy.7 = bf16[1,256,1024]{2,1,0:T(8,128)(2,1)} copy(bf16[1,256,1024]{2,1,0:T(8,128)(2,1)} %bitcast.3) | data formatting | bytes 1048576
  84.3 1.5 %copy.8 = f32[16,1024]{1,0:T(8,128)} copy(f32[16,1024]{1,0:T(8,128)} %get-tuple-element.9) | data formatting | bytes 131072

commit v2 on v1

v2 whole, which is shorter than its diff:
```python
import jax
import jax.numpy as jnp
from jax import lax
from jax.experimental import pallas as pl
from jax.experimental.pallas import tpu as pltpu
from jax.sharding import PartitionSpec as P

EPSILON = 1e-06
MESH = pl.DeviceIdType.MESH
BF16 = jnp.bfloat16
F32 = jnp.float32
ROWS = 256
FEAT = 1024
NZ, NY, NX, NCLIP = 16, 4, 4, 8
CHAINS = 32
PARTS = 2
PART = ROWS // PARTS
FAR = ((0, 0), (0, 1), (2, 0), (2, 1))
STEP = 32


def dot_nn(a, b):
    return jnp.dot(a, b, preferred_element_type=F32)


def dot_nt(a, b):
    return lax.dot_general(a, b, (((1,), (1,)), ((), ())), preferred_element_type=F32)


def kernel(
    h_ref, t_ref, w_ref, hg_ref, wg_ref,
    wv, hr, tr, su, tu, proj, inv, ds, e_near, e_far, acc, pall, ht,
    early, ws, wr, a0, a1, r0, r1, b0, b1, s0, s1, zs, zr, ag, pf, hgv, ov,
    load_sem, store_sem, halo_s, halo_r, fwd_s, fwd_r, pf_s, pf_r,
    d2d_s, d2d_r, st1_s, st1_r, st1b_s, st1b_r, st2_s, st2_r, z_s, z_r, ag_s, ag_r,
):
    k = lax.axis_index("clip")
    b = lax.axis_index("tok")
    c = lax.rem(b, 2)
    q = b // 2
    z = lax.rem(q, NZ)
    xl = q // NZ
    y = k // 2
    xh = lax.rem(k, 2)
    x = xh * 2 + xl
    has = (q > 0, q < CHAINS - 1)
    turn = (q == NZ, q == NZ - 1)

    def at(yy, xx, zz, cc):
        return {"clip": yy * 2 + xx // 2, "tok": lax.rem(xx, 2) * 32 + zz * 2 + cc}

    sib = {"clip": k, "tok": b + 1 - 2 * c}
    side = ({"clip": k, "tok": b - 2}, {"clip": k, "tok": b + 2})

    def y_peer(d):
        return at(lax.rem(y + d, NY), x, z, c)

    def x_peer(d):
        return at(y, lax.rem(x + d, NX), z, c)

    def z_peer(d):
        return at(y, x, lax.rem(z + d, NZ), c)

    def clip_peer(d):
        return {"clip": lax.rem(k + d, NCLIP), "tok": b}

    def remote(src, dst, ssem, rsem, dev):
        return pltpu.make_async_remote_copy(
            src_ref=src, dst_ref=dst, send_sem=ssem, recv_sem=rsem, device_id=dev, device_id_type=MESH
        )

    loads = [
        pltpu.make_async_copy(h_ref, hr.at[1], load_sem.at[0]),
        pltpu.make_async_copy(t_ref, tr, load_sem.at[1]),
        pltpu.make_async_copy(w_ref, wv, load_sem.at[2]),
    ]
    for cp in loads:
        cp.start()
    barrier = pltpu.get_barrier_semaphore()

    def greet(dev):
        pl.semaphore_signal(barrier, inc=1, device_id=dev, device_id_type=MESH)

    greet(sib)
    for i in range(2):
        @pl.when(has[i])
        def _(i=i):
            greet(side[i])
    greet(x_peer(1))
    greet(x_peer(3))
    for d in range(1, NCLIP):
        greet(clip_peer(d))
    for d in range(1, NZ):
        greet(z_peer(d))
    ends = jnp.where(q > 0, 1, 0) + jnp.where(q < CHAINS - 1, 1, 0)

    def teacher_unit():
        def body(i, carry):
            rows = pl.ds(pl.multiple_of(i * STEP, STEP), STEP)
            v = tr[rows].astype(F32)
            r = lax.rsqrt(jnp.sum(v * v, axis=-1, keepdims=True) + EPSILON)
            tu[1, 0, rows] = (v * r).astype(BF16)
            return carry

        lax.fori_loop(0, ROWS // STEP, body, 0)

    def student_unit(slot, first, n):
        rows_all = slice(first, first + n)
        for nb in range(4):
            cols = slice(nb * 256, (nb + 1) * 256)
            proj[slot, rows_all, cols] = dot_nn(hr[slot, rows_all], wv[:, cols])

        def body(i, carry):
            rows = pl.ds(pl.multiple_of(first + i * STEP, STEP), STEP)
            v = proj[slot, rows]
            r = lax.rsqrt(jnp.sum(v * v, axis=-1, keepdims=True) + EPSILON)
            inv[slot, rows] = jnp.broadcast_to(r, (STEP, 128))
            su[slot, 0, rows] = (v * r).astype(BF16)
            return carry

        lax.fori_loop(0, n // STEP, body, 0)

    def transposed(slot):
        for j in range(4):
            cols = slice(j * 256, (j + 1) * 256)
            v = hr[slot, :, cols].astype(F32).T.reshape(8, 2, 16, ROWS)
            for cc in range(2):
                ht[cc, j * 128 : (j + 1) * 128, slot * 256 : (slot + 1) * 256] = (
                    v[:, cc].reshape(128, ROWS).astype(BF16)
                )

    loads[0].wait()
    pl.semaphore_wait(barrier, 3 + (NCLIP - 1) + (NZ - 1) + ends)

    def part(n):
        return pl.ds(n * PART, PART)

    def halo_copies(i):
        slot = 2 - 2 * i
        copies = []
        for n in range(PARTS):
            copies.append(
                remote(hr.at[1, part(n)], hr.at[slot, part(n)], halo_s.at[i, n], halo_r.at[i, n], side[i])
            )
        for n in range(PARTS):
            m = PARTS + n
            copies.append(
                remote(tu.at[1, 0, part(n)], tu.at[slot, 0, part(n)], halo_s.at[i, m], halo_r.at[i, m], side[i])
            )
        return copies

    halo = [halo_copies(0), halo_copies(1)]

    def halo_send(n):
        for i in range(2):
            @pl.when(has[i])
            def _(i=i):
                halo[i][n].start()

    def halo_arrival(slot, n):
        i = slot // 2

        @pl.when(has[i])
        def _():
            halo[1 - i][n].wait_recv()

        @pl.when(jnp.logical_not(has[i]))
        def _():
            if n < PARTS:
                hr[slot, n * PART : (n + 1) * PART] = jnp.zeros((PART, FEAT), BF16)
            else:
                tu[slot, 0, (n - PARTS) * PART : (n - PARTS + 1) * PART] = jnp.zeros((PART, FEAT), BF16)

    for n in range(PARTS):
        halo_send(n)
    loads[1].wait()
    teacher_unit()
    for n in range(PARTS):
        halo_send(PARTS + n)
    loads[2].wait()
    student_unit(1, 0, ROWS)

    fwd = []

    def forward(src, dst, n):
        cp = remote(src, dst, fwd_s.at[n], fwd_r.at[n], sib)
        cp.start()
        fwd.append(cp)
        return cp

    own_fwd = [
        forward(tu.at[1, 0], tu.at[1, 1], 0),
        forward(su.at[1, 0], su.at[1, 1], 1),
    ]
    transposed(1)
    for cp in own_fwd:
        cp.wait_recv()

    acc[...] = jnp.zeros_like(acc)

    def weigh(slot, student, teacher):
        w = (256.0 * (student - teacher)).astype(BF16)
        p = w.astype(F32) * student
        s = p[:, :128]
        if p.shape[1] == 256:
            s = s + p[:, 128:]
        acc[slot] = acc[slot] + s
        return w

    for who in range(2):
        e_near[:, who * 256 : (who + 1) * 256] = weigh(
            1, dot_nt(su[1, 0], su[1, who]), dot_nt(tu[1, 0], tu[1, who])
        )

    s_fwd = []
    for n in range(PARTS):
        for slot in (0, 2):
            halo_arrival(slot, n)
            student_unit(slot, n * PART, PART)
            if n == PARTS - 1:
                s_fwd.append(forward(su.at[slot, 0], su.at[slot, 1], 2 + slot // 2))
    for slot in (0, 2):
        transposed(slot)
    for cp in s_fwd:
        cp.wait_recv()
    for j, (slot, who) in enumerate(FAR):
        ds[j] = dot_nt(su[1, 0], su[slot, who])
    for f in range(2):
        ds[4 + f] = dot_nt(su[2 * f, 0], su[2 - 2 * f, 0])
    xs = 2 - 2 * c
    xo = 2 * c
    ds[6] = dot_nt(su[xs, 0], su[xo, 1])

    def near_part(j, n):
        slot, who = FAR[j]
        lo = 512 + n * 4 * PART + j * PART
        e_near[:, lo : lo + PART] = weigh(
            1, ds[j, :, n * PART : (n + 1) * PART], dot_nt(tu[1, 0], tu[slot, who, n * PART : (n + 1) * PART])
        )

    def near_rows(n, cols):
        return jnp.concatenate([su[slot, who, n * PART : (n + 1) * PART, cols] for slot, who in FAR], axis=0)

    t_fwd = []
    for n in range(PARTS):
        for slot in (0, 2):
            halo_arrival(slot, PARTS + n)
            t_fwd.append(
                forward(tu.at[slot, 0, part(n)], tu.at[slot, 1, part(n)], 4 + n * 2 + slot // 2)
            )
        for j in (0, 2):
            near_part(j, n)
        if n == PARTS - 1:
            for f in range(2):
                e_far[f] = weigh(2 * f, ds[4 + f], dot_nt(tu[2 * f, 0], tu[2 - 2 * f, 0]))
        for cp in t_fwd[2 * n : 2 * n + 2]:
            cp.wait_recv()
        for j in (1, 3):
            near_part(j, n)
        if n == 0:
            for nb in range(4):
                cols = slice(nb * 256, (nb + 1) * 256)
                early[nb] = dot_nn(e_near[:, 0:512], su[1, :, :, cols].reshape(512, 256)) + dot_nn(
                    e_near[:, 512:1024], near_rows(0, cols)
                )
    e_far[2] = weigh(xs, ds[6], dot_nt(tu[xs, 0], tu[xo, 1]))

    def finish_along(i, carry):
        for slot in range(3):
            rows = pl.ds(pl.multiple_of(i * 64, 64), 64)
            along = jnp.sum(acc[slot, rows], axis=-1, keepdims=True)
            acc[slot, rows] = along * inv[slot, rows]
        return carry

    lax.fori_loop(0, ROWS // 64, finish_along, 0)

    back = [[None] * 4 for _ in range(2)]
    d2d, st1, st1b = [], [], []

    sent_first = (0, 1, 2)

    def send_turn(ds_):
        for i in range(2):
            @pl.when(turn[i])
            def _(i=i):
                for d in ds_:
                    back[i][d].start()

    def gradient(d):
        yy = lax.rem(y + 1 + d, NY)
        cols = pl.ds(pl.multiple_of(yy * 256, 256), 256)
        grads = {
            1: early[yy] + dot_nn(e_near[:, 1024:1536], near_rows(1, cols)),
            0: dot_nn(e_far[0], su[2, 0, :, cols]),
            2: dot_nn(e_far[1], su[0, 0, :, cols]),
        }
        cross = dot_nn(e_far[2], su[xo, 1, :, cols])
        first = jnp.where(c == 1, 1.0, 0.0)
        grads[0] = grads[0] + first * cross
        grads[2] = grads[2] + (1.0 - first) * cross
        for slot in (0, 2, 1):
            for i in range(2):
                at_cols = pl.ds(pl.multiple_of(yy * 256 + i * 128, 128), 128)
                v = grads[slot][:, i * 128 : (i + 1) * 128]
                v = (v - proj[slot, :, at_cols] * acc[slot]) * inv[slot]
                pall[yy, slot * ROWS : (slot + 1) * ROWS, i * 128 : (i + 1) * 128] = v.astype(BF16)
        for i in range(2):
            back[i][d] = remote(
                pall.at[yy, pl.ds(2 * i * ROWS, ROWS)], pf.at[1 - i, yy], pf_s.at[i, d], pf_r.at[i, d], side[i]
            )
            if d in sent_first:
                go = has[i]
            else:
                go = jnp.logical_and(has[i], jnp.logical_not(turn[i]))

            @pl.when(go)
            def _(i=i):
                back[i][d].start()

    def weight_sibling(d):
        yy = lax.rem(y + 1 + d, NY)
        part_sib = dot_nn(ht[1 - c], pall[yy])
        for i in range(2):
            ws[d, i] = part_sib[:, i * 128 : (i + 1) * 128].astype(BF16)
        cp = remote(ws.at[d], wr.at[d], d2d_s.at[d], d2d_r.at[d], sib)
        cp.start()
        d2d.append(cp)

    def reduce_first(d):
        dy = (1 + d) % 4
        yy = lax.rem(y + dy, NY)
        part_own = dot_nn(ht[c], pall[yy])
        d2d[d].wait_recv()
        for i in range(2):
            v = (part_own[:, i * 128 : (i + 1) * 128] + wr[d, i].astype(F32)).astype(BF16)
            for j in range(2):
                a0[yy, i * 2 + j] = v[j * 256 : j * 256 + 128]
                a1[i * 2 + j, yy] = v[j * 256 + 128 : j * 256 + 256]
        if dy:
            cp = remote(a0.at[yy], r0.at[dy - 1], st1_s.at[dy - 1], st1_r.at[dy - 1], y_peer(dy))
            cp.start()
            st1.append(cp)
        for dx in range(1, NX):
            xx = lax.rem(x + dx, NX)
            cp = remote(
                a1.at[xx, yy], r1.at[dx - 1, yy], st1b_s.at[dx - 1, dy], st1b_r.at[dx - 1, dy], x_peer(dx)
            )
            cp.start()
            st1b.append(cp)

    gradient(0)
    weight_sibling(0)
    for d in range(2):
        gradient(d + 1)
        reduce_first(d)
        weight_sibling(d + 1)
    gradient(3)
    weight_sibling(3)
    reduce_first(2)
    reduce_first(3)

    st2 = []
    for cp in st1:
        cp.wait_recv()
    for dx in (1, 2, 3, 0):
        xx = lax.rem(x + dx, NX)
        v = a0[y, xx].astype(F32)
        for i in range(3):
            v = v + r0[i, xx].astype(F32)
        b0[xx] = v.astype(BF16)
        if dx:
            cp = remote(b0.at[xx], s0.at[dx - 1], st2_s.at[0, dx - 1], st2_r.at[0, dx - 1], x_peer(dx))
            cp.start()
            st2.append(cp)
    for cp in st1b:
        cp.wait_recv()
    send_turn(())
    for dy in (1, 2, 3, 0):
        yy = lax.rem(y + dy, NY)
        v = a1[x, yy].astype(F32)
        for i in range(3):
            v = v + r1[i, yy].astype(F32)
        b1[yy] = v.astype(BF16)
        if dy:
            cp = remote(b1.at[yy], s1.at[dy - 1], st2_s.at[1, dy - 1], st2_r.at[1, dy - 1], y_peer(dy))
            cp.start()
            st2.append(cp)
    def over_z(half, own, got, copies):
        for cp in copies:
            cp.wait_recv()
        v = own.astype(F32)
        for i in range(3):
            v = v + got[i].astype(F32)
        zs[half * 8 : half * 8 + 8] = v.reshape(8, 16, 128).astype(BF16)
        for zz in range(half * 8, half * 8 + 8):
            cp = remote(zs.at[zz], zr.at[z], z_s.at[zz], z_r.at[z], at(y, x, zz, c))
            zc.append(cp)

            @pl.when(z != zz)
            def _(cp=cp):
                cp.start()

    zc = []
    over_z(0, b0[x], s0, st2[:3])
    over_z(1, b1[y], s1, st2[3:])
    send_turn((3,))
    zr[z] = zs[z]

    def hidden_gradient():
        for i in range(2):
            @pl.when(has[i])
            def _(i=i):
                for d in range(4):
                    back[1 - i][d].wait_recv()

            @pl.when(jnp.logical_not(has[i]))
            def _(i=i):
                pf[i] = jnp.zeros((4, ROWS, 256), BF16)

        for nb in range(4):
            v = pall[nb, ROWS : 2 * ROWS].astype(F32) + pf[0, nb].astype(F32) + pf[1, nb].astype(F32)
            hgv[:, nb * 256 : (nb + 1) * 256] = v.astype(BF16)
        for nb in range(4):
            cols = slice(nb * 256, (nb + 1) * 256)
            ov[:, cols] = dot_nt(hgv[...], wv[nb * 256 : (nb + 1) * 256]).astype(BF16)

    def weight_gather():
        for zz in range(NZ):
            @pl.when(z != zz)
            def _(zz=zz):
                remote(zs.at[zz], zr.at[zz], z_s.at[zz], z_r.at[zz], at(y, x, zz, c)).wait_recv()

        v = zr[0].astype(F32)
        for zz in range(1, NZ):
            v = v + zr[zz].astype(F32)
        ag[k] = v * (1.0 / 1024.0)
        copies = []
        for d in range(1, NCLIP):
            cp = remote(ag.at[k], ag.at[k], ag_s.at[d - 1], ag_r.at[d - 1], clip_peer(d))
            cp.start()
            copies.append(cp)
        return copies

    agc = weight_gather()
    hidden_gradient()
    store = pltpu.make_async_copy(ov, hg_ref, store_sem.at[0])
    store.start()
    for cp in agc:
        cp.wait_recv()
    for i in range(NCLIP):
        wg_ref[:, i * 128 : (i + 1) * 128] = ag[i]

    for i in range(2):
        @pl.when(has[i])
        def _(i=i):
            for cp in halo[i] + back[i]:
                cp.wait_send()
    for zz in range(NZ):
        @pl.when(z != zz)
        def _(zz=zz):
            zc[zz].wait_send()

    for cp in fwd + d2d + st1 + st1b + st2 + agc:
        cp.wait_send()
    store.wait()


def handed_on(hg_in, wg_in, hg_out, wg_out):
    hg_out[...] = hg_in[...]
    wg_out[...] = wg_in[...]


def local(student_hidden, teacher_tokens, proj_weight):
    dma = pltpu.SemaphoreType.DMA
    vm = pltpu.VMEM
    anywhere = pl.BlockSpec(memory_space=pl.ANY)
    results = (
        jax.ShapeDtypeStruct((ROWS, FEAT), BF16),
        jax.ShapeDtypeStruct((16, FEAT), F32),
    )
    made = pl.pallas_call(
        kernel,
        out_shape=results,
        in_specs=[anywhere] * 3,
        out_specs=(anywhere, pl.BlockSpec(memory_space=pltpu.VMEM)),
        scratch_shapes=[
            vm((FEAT, FEAT), BF16),
            vm((3, ROWS, FEAT), BF16),
            vm((ROWS, FEAT), BF16),
            vm((3, 2, ROWS, FEAT), BF16),
            vm((3, 2, ROWS, FEAT), BF16),
            vm((3, ROWS, FEAT), F32),
            vm((3, ROWS, 128), F32),
            vm((7, ROWS, ROWS), F32),
            vm((ROWS, 6 * ROWS), BF16),
            vm((3, ROWS, ROWS), BF16),
            vm((3, ROWS, 128), F32),
            vm((4, 3 * ROWS, 256), BF16),
            vm((2, 512, 3 * ROWS), BF16),
            vm((4, ROWS, 256), F32),
            vm((4, 2, 512, 128), BF16),
            vm((4, 2, 512, 128), BF16),
            vm((4, 4, 128, 128), BF16),
            vm((4, 4, 128, 128), BF16),
            vm((3, 4, 128, 128), BF16),
            vm((3, 4, 128, 128), BF16),
            vm((4, 128, 128), BF16),
            vm((4, 128, 128), BF16),
            vm((3, 128, 128), BF16),
            vm((3, 128, 128), BF16),
            vm((NZ, 16, 128), BF16),
            vm((NZ, 16, 128), BF16),
            vm((NCLIP, 16, 128), F32),
            vm((2, 4, ROWS, 256), BF16),
            vm((ROWS, FEAT), BF16),
            vm((ROWS, FEAT), BF16),
            dma((3,)), dma((1,)),
            dma((2, 2 * PARTS)), dma((2, 2 * PARTS)),
            dma((4 + 2 * PARTS,)), dma((4 + 2 * PARTS,)),
            dma((2, 4)), dma((2, 4)),
            dma((4,)), dma((4,)),
            dma((3,)), dma((3,)),
            dma((3, 4)), dma((3, 4)),
            dma((2, 3)), dma((2, 3)),
            dma((NZ,)), dma((NZ,)),
            dma((NCLIP - 1,)), dma((NCLIP - 1,)),
        ],
        compiler_params=pltpu.CompilerParams(
            collective_id=0, has_side_effects=True, vmem_limit_bytes=56 * 2**20
        ),
    )(student_hidden[0], teacher_tokens[0], proj_weight)
    hidden_grad, weight_grad = pl.pallas_call(
        handed_on,
        out_shape=results,
        in_specs=[pl.BlockSpec(memory_space=pltpu.VMEM)] * 2,
        out_specs=(pl.BlockSpec(memory_space=pltpu.VMEM),) * 2,
    )(*made)
    return hidden_grad[None], weight_grad


def solution(mesh):
    placed = (P("clip", "tok", None), P("clip", "tok", None), P())
    return jax.shard_map(
        local,
        mesh=mesh,
        in_specs=placed,
        out_specs=(P("clip", "tok", None), P("tok", None)),
        check_vma=False,
    )
```

time: 85.9 us -> 75.8 us (0.88)
  the two profiles are of different devices: /device:TPU:32 before, /device:TPU:4 now
where the time goes in v2:
time: 75.8 us; the launch traced here: 75.6 us
  Pallas kernels  75 us (99%)
    pallas_call x1, Pallas kernels, local(): pl.pallas_call(kernel, out_shape=results, in_specs=[anywhere] * 3, out_sp...  73.1 us
    pallas_call x1, Pallas kernels, local(): pl.pallas_call(handed_on, out_shape=results, in_specs=[pl.BlockSpec(memor...  1.88 us

profile of v2, /device:TPU:4, one launch (start us, length us, event | category | flops | bytes accessed | tf_op | source)
XLA Modules:
  0.0 75.6 jit_solution(2835900019263527272)
XLA Ops:
  0.6 73.1 %shard_map.50 = (bf16[256,1024]{1,0:T(8,128)(2,1)}, f32[16,1024]{1,0:T(8,128)}) custom-call(bf16[256,1024]{1,0:T(8,128)(2,1)} %bitcast.3, bf16[256,1024]{1,0:T(8,128)(2,1)} %bitcast.4, bf16[1024,1024]{1,0:T(8,128)(2,1)} %w_ref.1), custom_call_target="tpu_custom_call" | custom-call | tf_op jit(solution)/shard_map/pallas_call | solution.py:481
  73.7 1.9 %shard_map.51 = (bf16[256,1024]{1,0:T(8,128)(2,1)}, f32[16,1024]{1,0:T(8,128)}) custom-call(bf16[256,1024]{1,0:T(8,128)(2,1)} %get-tuple-element.6.hg_in, f32[16,1024]{1,0:T(8,128)} %get-tuple-element.7.wg_in), custom_call_target="tpu_custom_call" | custom-call | tf_op jit(solution)/shard_map/pallas_call | solution.py:532

commit v3 on v2

--- a/solution.py
+++ b/solution.py
@@ -15,6 +15,7 @@
 CHAINS = 32
 PARTS = 2
 PART = ROWS // PARTS
+WORDS = 7
 FAR = ((0, 0), (0, 1), (2, 0), (2, 1))
 STEP = 32
 
@@ -32,7 +33,7 @@
     wv, hr, tr, su, tu, proj, inv, ds, e_near, e_far, acc, pall, ht,
     early, ws, wr, a0, a1, r0, r1, b0, b1, s0, s1, zs, zr, ag, pf, hgv, ov,
     load_sem, store_sem, halo_s, halo_r, fwd_s, fwd_r, pf_s, pf_r,
-    d2d_s, d2d_r, st1_s, st1_r, st1b_s, st1b_r, st2_s, st2_r, z_s, z_r, ag_s, ag_r,
+    d2d_s, d2d_r, st1_s, st1_r, st1b_s, st1b_r, st2_s, st2_r, z_s, z_r, ag_s, ag_r, word,
 ):
     k = lax.axis_index("clip")
     b = lax.axis_index("tok")
@@ -45,6 +46,7 @@
     x = xh * 2 + xl
     has = (q > 0, q < CHAINS - 1)
     turn = (q == NZ, q == NZ - 1)
+    corner = (2 * CHAINS - 2 + c, c)
 
     def at(yy, xx, zz, cc):
         return {"clip": yy * 2 + xx // 2, "tok": lax.rem(xx, 2) * 32 + zz * 2 + cc}
@@ -60,9 +62,6 @@
 
     def z_peer(d):
         return at(y, x, lax.rem(z + d, NZ), c)
-
-    def clip_peer(d):
-        return {"clip": lax.rem(k + d, NCLIP), "tok": b}
 
     def remote(src, dst, ssem, rsem, dev):
         return pltpu.make_async_remote_copy(
@@ -81,18 +80,28 @@
     def greet(dev):
         pl.semaphore_signal(barrier, inc=1, device_id=dev, device_id_type=MESH)
 
-    greet(sib)
+    near_peers = (
+        at(y, x, lax.rem(z + 1, NZ), c), at(y, x, lax.rem(z + NZ - 1, NZ), c),
+        y_peer(1), y_peer(NY - 1), x_peer(1), x_peer(NX - 1),
+    )
     for i in range(2):
         @pl.when(has[i])
         def _(i=i):
             greet(side[i])
-    greet(x_peer(1))
-    greet(x_peer(3))
-    for d in range(1, NCLIP):
-        greet(clip_peer(d))
-    for d in range(1, NZ):
-        greet(z_peer(d))
+    greet(sib)
+    for dev in near_peers:
+        greet(dev)
     ends = jnp.where(q > 0, 1, 0) + jnp.where(q < CHAINS - 1, 1, 0)
+
+    def heard(n):
+        for i in range(len(near_peers)):
+            pl.semaphore_wait(word.at[n, i], 1)
+
+    def pass_on(n):
+        if n:
+            heard(n - 1)
+        for i, dev in enumerate(near_peers):
+            pl.semaphore_signal(word.at[n, i], inc=1, device_id=dev, device_id_type=MESH)
 
     def teacher_unit():
         def body(i, carry):
@@ -106,9 +115,13 @@
 
     def student_unit(slot, first, n):
         rows_all = slice(first, first + n)
-        for nb in range(4):
-            cols = slice(nb * 256, (nb + 1) * 256)
+
+        def block(nb, carry):
+            cols = pl.ds(pl.multiple_of(nb * 256, 256), 256)
             proj[slot, rows_all, cols] = dot_nn(hr[slot, rows_all], wv[:, cols])
+            return carry
+
+        lax.fori_loop(0, 4, block, 0)
 
         def body(i, carry):
             rows = pl.ds(pl.multiple_of(first + i * STEP, STEP), STEP)
@@ -130,26 +143,20 @@
                 )
 
     loads[0].wait()
-    pl.semaphore_wait(barrier, 3 + (NCLIP - 1) + (NZ - 1) + ends)
+    pl.semaphore_wait(barrier, 1 + len(near_peers) + ends)
 
     def part(n):
         return pl.ds(n * PART, PART)
 
-    def halo_copies(i):
+    def halo_copy(i, n):
         slot = 2 - 2 * i
-        copies = []
-        for n in range(PARTS):
-            copies.append(
-                remote(hr.at[1, part(n)], hr.at[slot, part(n)], halo_s.at[i, n], halo_r.at[i, n], side[i])
-            )
-        for n in range(PARTS):
-            m = PARTS + n
-            copies.append(
-                remote(tu.at[1, 0, part(n)], tu.at[slot, 0, part(n)], halo_s.at[i, m], halo_r.at[i, m], side[i])
-            )
-        return copies
-
-    halo = [halo_copies(0), halo_copies(1)]
+        sems = (halo_s.at[i, n], halo_r.at[i, n], side[i])
+        if isinstance(n, int) and n < PARTS:
+            return remote(hr.at[1, part(n)], hr.at[slot, part(n)], *sems)
+        rows = pl.ds(pl.multiple_of((n - PARTS) * PART, PART), PART)
+        return remote(tu.at[1, 0, rows], tu.at[slot, 0, rows], *sems)
+
+    halo = [[halo_copy(i, n) for n in range(2 * PARTS)] for i in range(2)]
 
     def halo_send(n):
         for i in range(2):
@@ -166,19 +173,18 @@
 
         @pl.when(jnp.logical_not(has[i]))
         def _():
-            if n < PARTS:
-                hr[slot, n * PART : (n + 1) * PART] = jnp.zeros((PART, FEAT), BF16)
-            else:
-                tu[slot, 0, (n - PARTS) * PART : (n - PARTS + 1) * PART] = jnp.zeros((PART, FEAT), BF16)
+            hr[slot, n * PART : (n + 1) * PART] = jnp.zeros((PART, FEAT), BF16)
 
     for n in range(PARTS):
         halo_send(n)
+    pass_on(0)
     loads[1].wait()
     teacher_unit()
     for n in range(PARTS):
         halo_send(PARTS + n)
     loads[2].wait()
     student_unit(1, 0, ROWS)
+    pass_on(1)
 
     fwd = []
 
@@ -212,6 +218,8 @@
             1, dot_nt(su[1, 0], su[1, who]), dot_nt(tu[1, 0], tu[1, who])
         )
 
+    pass_on(2)
+
     s_fwd = []
     for n in range(PARTS):
         for slot in (0, 2):
@@ -219,51 +227,105 @@
             student_unit(slot, n * PART, PART)
             if n == PARTS - 1:
                 s_fwd.append(forward(su.at[slot, 0], su.at[slot, 1], 2 + slot // 2))
+            pass_on(3 + n * 2 + slot // 2)
     for slot in (0, 2):
         transposed(slot)
     for cp in s_fwd:
         cp.wait_recv()
-    for j, (slot, who) in enumerate(FAR):
-        ds[j] = dot_nt(su[1, 0], su[slot, who])
-    for f in range(2):
-        ds[4 + f] = dot_nt(su[2 * f, 0], su[2 - 2 * f, 0])
     xs = 2 - 2 * c
     xo = 2 * c
-    ds[6] = dot_nt(su[xs, 0], su[xo, 1])
+
+    def far_pair(f):
+        rows = jnp.where(f == 2, xs, 2 * f)
+        return rows, 2 - rows, jnp.where(f == 2, 1, 0)
+
+    def near_student(j, carry):
+        ds[j] = dot_nt(su[1, 0], su[(j // 2) * 2, lax.rem(j, 2)])
+        return carry
+
+    lax.fori_loop(0, 4, near_student, 0)
+
+    def far_student(f, carry):
+        rows, slot, who = far_pair(f)
+        ds[4 + f] = dot_nt(su[rows, 0], su[slot, who])
+        return carry
+
+    lax.fori_loop(0, 3, far_student, 0)
 
     def near_part(j, n):
-        slot, who = FAR[j]
-        lo = 512 + n * 4 * PART + j * PART
-        e_near[:, lo : lo + PART] = weigh(
-            1, ds[j, :, n * PART : (n + 1) * PART], dot_nt(tu[1, 0], tu[slot, who, n * PART : (n + 1) * PART])
+        at_rows = pl.ds(pl.multiple_of(n * PART, PART), PART)
+        e_near[:, pl.ds(pl.multiple_of(512 + n * 4 * PART + j * PART, PART), PART)] = weigh(
+            1, ds[j, :, at_rows], dot_nt(tu[1, 0], tu[(j // 2) * 2, lax.rem(j, 2), at_rows])
         )
 
     def near_rows(n, cols):
         return jnp.concatenate([su[slot, who, n * PART : (n + 1) * PART, cols] for slot, who in FAR], axis=0)
 
-    t_fwd = []
-    for n in range(PARTS):
-        for slot in (0, 2):
-            halo_arrival(slot, PARTS + n)
-            t_fwd.append(
-                forward(tu.at[slot, 0, part(n)], tu.at[slot, 1, part(n)], 4 + n * 2 + slot // 2)
-            )
-        for j in (0, 2):
-            near_part(j, n)
-        if n == PARTS - 1:
-            for f in range(2):
-                e_far[f] = weigh(2 * f, ds[4 + f], dot_nt(tu[2 * f, 0], tu[2 - 2 * f, 0]))
-        for cp in t_fwd[2 * n : 2 * n + 2]:
+    def teacher_part(n, carry):
+        def arrived(slot):
+            i = slot // 2
+            rows = pl.ds(pl.multiple_of(n * PART, PART), PART)
+
+            @pl.when(has[i])
+            def _():
+                halo_copy(1 - i, PARTS + n).wait_recv()
+
+            @pl.when(jnp.logical_not(has[i]))
+            def _():
+                tu[slot, 0, rows] = jnp.zeros((PART, FEAT), BF16)
+
+            cp = teacher_forward(slot, n)
+            cp.start()
+            return cp
+
+        copies = [arrived(0), arrived(2)]
+
+        def direct(j, cc):
+            near_part(2 * j, n)
+            return cc
+
+        def handed(j, cc):
+            near_part(2 * j + 1, n)
+            return cc
+
+        lax.fori_loop(0, 2, direct, 0)
+
+        @pl.when(n == PARTS - 1)
+        def _():
+            lax.fori_loop(0, 2, far_weight, 0)
+
+        for cp in copies:
             cp.wait_recv()
-        for j in (1, 3):
-            near_part(j, n)
-        if n == 0:
-            for nb in range(4):
-                cols = slice(nb * 256, (nb + 1) * 256)
+        lax.fori_loop(0, 2, handed, 0)
+
+        @pl.when(n == 0)
+        def _():
+            def block(nb, cc):
+                cols = pl.ds(pl.multiple_of(nb * 256, 256), 256)
                 early[nb] = dot_nn(e_near[:, 0:512], su[1, :, :, cols].reshape(512, 256)) + dot_nn(
                     e_near[:, 512:1024], near_rows(0, cols)
                 )
-    e_far[2] = weigh(xs, ds[6], dot_nt(tu[xs, 0], tu[xo, 1]))
+                return cc
+
+            lax.fori_loop(0, 4, block, 0)
+
+        return carry
+
+    def teacher_forward(slot, n):
+        rows = pl.ds(pl.multiple_of(n * PART, PART), PART)
+        m = 4 + n * 2 + slot // 2
+        return remote(tu.at[slot, 0, rows], tu.at[slot, 1, rows], fwd_s.at[m], fwd_r.at[m], sib)
+
+    def far_weight(f, carry):
+        rows, slot, who = far_pair(f)
+        e_far[f] = weigh(rows, ds[4 + f], dot_nt(tu[rows, 0], tu[slot, who]))
+        return carry
+
+    lax.fori_loop(0, PARTS, teacher_part, 0)
+    far_weight(2, 0)
+    for n in range(PARTS):
+        for slot in (0, 2):
+            fwd.append(teacher_forward(slot, n))
 
     def finish_along(i, carry):
         for slot in range(3):
@@ -274,20 +336,47 @@
 
     lax.fori_loop(0, ROWS // 64, finish_along, 0)
 
-    back = [[None] * 4 for _ in range(2)]
-    d2d, st1, st1b = [], [], []
-
-    sent_first = (0, 1, 2)
-
-    def send_turn(ds_):
+    heard(WORDS - 1)
+
+    def offset(d):
+        return jnp.where(d == 0, 2, jnp.where(d == 1, 1, jnp.where(d == 2, 3, 0)))
+
+    def chunk(d):
+        return lax.rem(y + offset(d), NY)
+
+    def back_copy(i, d):
+        yy = chunk(d)
+        dev = {"clip": k, "tok": jnp.where(jnp.logical_and(turn[i], lax.rem(d, 2) == 1), corner[i], b + 4 * i - 2)}
+        return remote(
+            pall.at[yy, pl.ds(2 * i * ROWS, ROWS)], pf.at[1 - i, yy], pf_s.at[i, d], pf_r.at[i, d], dev
+        )
+
+    def relay_copy(i, d):
+        yy = chunk(d)
+        dev = {"clip": k, "tok": jnp.where(xl == 0, b + 32, b - 32)}
+        return remote(pf.at[i, yy], pf.at[i, yy], pf_s.at[i, d], pf_r.at[1 - i, d], dev)
+
+    def relay(d):
         for i in range(2):
-            @pl.when(turn[i])
+            @pl.when(jnp.logical_not(has[i]))
             def _(i=i):
-                for d in ds_:
-                    back[i][d].start()
+                relay_copy(i, d).wait_recv()
+                relay_copy(i, d).start()
+
+    def d2d_copy(d):
+        return remote(ws.at[d], wr.at[d], d2d_s.at[d], d2d_r.at[d], sib)
+
+    def first_y(d):
+        return remote(a0.at[chunk(d)], r0.at[d], st1_s.at[d], st1_r.at[d], y_peer(offset(d)))
+
+    def first_x(dx, d):
+        yy = chunk(d)
+        return remote(
+            a1.at[lax.rem(x + dx, NX), yy], r1.at[dx - 1, yy], st1b_s.at[dx - 1, d], st1b_r.at[dx - 1, d], x_peer(dx)
+        )
 
     def gradient(d):
-        yy = lax.rem(y + 1 + d, NY)
+        yy = chunk(d)
         cols = pl.ds(pl.multiple_of(yy * 256, 256), 256)
         grads = {
             1: early[yy] + dot_nn(e_near[:, 1024:1536], near_rows(1, cols)),
@@ -305,64 +394,56 @@
                 v = (v - proj[slot, :, at_cols] * acc[slot]) * inv[slot]
                 pall[yy, slot * ROWS : (slot + 1) * ROWS, i * 128 : (i + 1) * 128] = v.astype(BF16)
         for i in range(2):
-            back[i][d] = remote(
-                pall.at[yy, pl.ds(2 * i * ROWS, ROWS)], pf.at[1 - i, yy], pf_s.at[i, d], pf_r.at[i, d], side[i]
-            )
-            if d in sent_first:
-                go = has[i]
-            else:
-                go = jnp.logical_and(has[i], jnp.logical_not(turn[i]))
-
-            @pl.when(go)
+            @pl.when(has[i])
             def _(i=i):
-                back[i][d].start()
+                back_copy(i, d).start()
 
     def weight_sibling(d):
-        yy = lax.rem(y + 1 + d, NY)
-        part_sib = dot_nn(ht[1 - c], pall[yy])
+        part_sib = dot_nn(ht[1 - c], pall[chunk(d)])
         for i in range(2):
             ws[d, i] = part_sib[:, i * 128 : (i + 1) * 128].astype(BF16)
-        cp = remote(ws.at[d], wr.at[d], d2d_s.at[d], d2d_r.at[d], sib)
-        cp.start()
-        d2d.append(cp)
+        d2d_copy(d).start()
 
     def reduce_first(d):
-        dy = (1 + d) % 4
-        yy = lax.rem(y + dy, NY)
+        yy = chunk(d)
         part_own = dot_nn(ht[c], pall[yy])
-        d2d[d].wait_recv()
+        d2d_copy(d).wait_recv()
         for i in range(2):
             v = (part_own[:, i * 128 : (i + 1) * 128] + wr[d, i].astype(F32)).astype(BF16)
             for j in range(2):
                 a0[yy, i * 2 + j] = v[j * 256 : j * 256 + 128]
                 a1[i * 2 + j, yy] = v[j * 256 + 128 : j * 256 + 256]
-        if dy:
-            cp = remote(a0.at[yy], r0.at[dy - 1], st1_s.at[dy - 1], st1_r.at[dy - 1], y_peer(dy))
-            cp.start()
-            st1.append(cp)
-        for dx in range(1, NX):
-            xx = lax.rem(x + dx, NX)
-            cp = remote(
-                a1.at[xx, yy], r1.at[dx - 1, yy], st1b_s.at[dx - 1, dy], st1b_r.at[dx - 1, dy], x_peer(dx)
-            )
-            cp.start()
-            st1b.append(cp)
-
-    gradient(0)
-    weight_sibling(0)
-    for d in range(2):
-        gradient(d + 1)
-        reduce_first(d)
-        weight_sibling(d + 1)
-    gradient(3)
-    weight_sibling(3)
-    reduce_first(2)
-    reduce_first(3)
-
+
+        @pl.when(d < 3)
+        def _():
+            first_y(d).start()
+
+        for dx in (2, 1, 3):
+            first_x(dx, d).start()
+
+    def step(s, carry):
+        @pl.when(s < 4)
+        def _():
+            gradient(s)
+            weight_sibling(s)
+
+        @pl.when(s > 0)
+        def _():
+            reduce_first(s - 1)
+
+        return carry
+
+    lax.fori_loop(0, 5, step, 0)
+    back = [[back_copy(i, d) for d in range(4)] for i in range(2)]
+    d2d = [d2d_copy(d) for d in range(4)]
+    st1 = [first_y(d) for d in range(3)]
+    st1b = [first_x(dx, d) for dx in (1, 2, 3) for d in range(4)]
+
+    relay(1)
     st2 = []
     for cp in st1:
         cp.wait_recv()
-    for dx in (1, 2, 3, 0):
+    for dx in (2, 1, 3, 0):
         xx = lax.rem(x + dx, NX)
         v = a0[y, xx].astype(F32)
         for i in range(3):
@@ -374,8 +455,8 @@
             st2.append(cp)
     for cp in st1b:
         cp.wait_recv()
-    send_turn(())
-    for dy in (1, 2, 3, 0):
+    relay(3)
+    for dy in (2, 1, 3, 0):
         yy = lax.rem(y + dy, NY)
         v = a1[x, yy].astype(F32)
         for i in range(3):
@@ -385,26 +466,18 @@
             cp = remote(b1.at[yy], s1.at[dy - 1], st2_s.at[1, dy - 1], st2_r.at[1, dy - 1], y_peer(dy))
             cp.start()
             st2.append(cp)
-    def over_z(half, own, got, copies):
-        for cp in copies:
-            cp.wait_recv()
+    for cp in st2:
+        cp.wait_recv()
+    for half, own, got in ((0, b0[x], s0), (1, b1[y], s1)):
         v = own.astype(F32)
         for i in range(3):
             v = v + got[i].astype(F32)
         zs[half * 8 : half * 8 + 8] = v.reshape(8, 16, 128).astype(BF16)
-        for zz in range(half * 8, half * 8 + 8):
-            cp = remote(zs.at[zz], zr.at[z], z_s.at[zz], z_r.at[z], at(y, x, zz, c))
-            zc.append(cp)
-
-            @pl.when(z != zz)
-            def _(cp=cp):
-                cp.start()
-
     zc = []
-    over_z(0, b0[x], s0, st2[:3])
-    over_z(1, b1[y], s1, st2[3:])
-    send_turn((3,))
-    zr[z] = zs[z]
+    for d in (8, 7, 9, 6, 10, 5, 11, 4, 12, 3, 13, 2, 14, 1, 15):
+        cp = remote(zs.at[lax.rem(z + d, NZ)], zr.at[d - 1], z_s.at[d - 1], z_r.at[d - 1], z_peer(d))
+        cp.start()
+        zc.append(cp)
 
     def hidden_gradient():
         for i in range(2):
@@ -415,28 +488,32 @@
 
             @pl.when(jnp.logical_not(has[i]))
             def _(i=i):
+                for d in (1, 3):
+                    relay_copy(i, d).wait_send()
                 pf[i] = jnp.zeros((4, ROWS, 256), BF16)
 
         for nb in range(4):
             v = pall[nb, ROWS : 2 * ROWS].astype(F32) + pf[0, nb].astype(F32) + pf[1, nb].astype(F32)
             hgv[:, nb * 256 : (nb + 1) * 256] = v.astype(BF16)
-        for nb in range(4):
-            cols = slice(nb * 256, (nb + 1) * 256)
-            ov[:, cols] = dot_nt(hgv[...], wv[nb * 256 : (nb + 1) * 256]).astype(BF16)
+
+        def block(nb, carry):
+            at_block = pl.ds(pl.multiple_of(nb * 256, 256), 256)
+            ov[:, at_block] = dot_nt(hgv[...], wv[at_block]).astype(BF16)
+            return carry
+
+        lax.fori_loop(0, 4, block, 0)
 
     def weight_gather():
-        for zz in range(NZ):
-            @pl.when(z != zz)
-            def _(zz=zz):
-                remote(zs.at[zz], zr.at[zz], z_s.at[zz], z_r.at[zz], at(y, x, zz, c)).wait_recv()
-
-        v = zr[0].astype(F32)
-        for zz in range(1, NZ):
-            v = v + zr[zz].astype(F32)
+        v = zs[z].astype(F32)
+        for cp in zc:
+            cp.wait_recv()
+        for d in range(NZ - 1):
+            v = v + zr[d].astype(F32)
         ag[k] = v * (1.0 / 1024.0)
         copies = []
-        for d in range(1, NCLIP):
-            cp = remote(ag.at[k], ag.at[k], ag_s.at[d - 1], ag_r.at[d - 1], clip_peer(d))
+        for n, (dy, dh) in enumerate(((2, 1), (1, 1), (3, 1), (2, 0), (0, 1), (1, 0), (3, 0))):
+            dev = {"clip": lax.rem(y + dy, NY) * 2 + (1 - xh if dh else xh), "tok": b}
+            cp = remote(ag.at[k], ag.at[k], ag_s.at[n], ag_r.at[n], dev)
             cp.start()
             copies.append(cp)
         return copies
@@ -455,12 +532,7 @@
         def _(i=i):
             for cp in halo[i] + back[i]:
                 cp.wait_send()
-    for zz in range(NZ):
-        @pl.when(z != zz)
-        def _(zz=zz):
-            zc[zz].wait_send()
-
-    for cp in fwd + d2d + st1 + st1b + st2 + agc:
+    for cp in fwd + d2d + st1 + st1b + st2 + zc + agc:
         cp.wait_send()
     store.wait()
 
@@ -509,7 +581,7 @@
             vm((3, 128, 128), BF16),
             vm((3, 128, 128), BF16),
             vm((NZ, 16, 128), BF16),
-            vm((NZ, 16, 128), BF16),
+            vm((NZ - 1, 16, 128), BF16),
             vm((NCLIP, 16, 128), F32),
             vm((2, 4, ROWS, 256), BF16),
             vm((ROWS, FEAT), BF16),
@@ -522,8 +594,9 @@
             dma((3,)), dma((3,)),
             dma((3, 4)), dma((3, 4)),
             dma((2, 3)), dma((2, 3)),
-            dma((NZ,)), dma((NZ,)),
+            dma((NZ - 1,)), dma((NZ - 1,)),
             dma((NCLIP - 1,)), dma((NCLIP - 1,)),
+            pltpu.SemaphoreType.REGULAR((WORDS, 6)),
         ],
         compiler_params=pltpu.CompilerParams(
             collective_id=0, has_side_effects=True, vmem_limit_bytes=56 * 2**20

time: 75.8 us -> 72.9 us (0.962)
  the two profiles are of different devices: /device:TPU:4 before, /device:TPU:2 now
where the time goes in v3:
time: 72.9 us; the launch traced here: 72.8 us
  Pallas kernels  72.2 us (99%)
    pallas_call x1, Pallas kernels, local(): pl.pallas_call(kernel, out_shape=results, in_specs=[anywhere] * 3, out_sp...  70.3 us
    pallas_call x1, Pallas kernels, local(): pl.pallas_call(handed_on, out_shape=results, in_specs=[pl.BlockSpec(memor...  1.88 us

profile of v3, /device:TPU:2, one launch (start us, length us, event | category | flops | bytes accessed | tf_op | source)
XLA Modules:
  0.0 72.8 jit_solution(7516471169751808377)
XLA Ops:
  0.6 70.3 %shard_map.50 = (bf16[256,1024]{1,0:T(8,128)(2,1)}, f32[16,1024]{1,0:T(8,128)}) custom-call(bf16[256,1024]{1,0:T(8,128)(2,1)} %bitcast.3, bf16[256,1024]{1,0:T(8,128)(2,1)} %bitcast.4, bf16[1024,1024]{1,0:T(8,128)(2,1)} %w_ref.1), custom_call_target="tpu_custom_call" | custom-call | tf_op jit(solution)/shard_map/pallas_call | solution.py:553
  70.9 1.9 %shard_map.51 = (bf16[256,1024]{1,0:T(8,128)(2,1)}, f32[16,1024]{1,0:T(8,128)}) custom-call(bf16[256,1024]{1,0:T(8,128)(2,1)} %get-tuple-element.6.hg_in, f32[16,1024]{1,0:T(8,128)} %get-tuple-element.7.wg_in), custom_call_target="tpu_custom_call" | custom-call | tf_op jit(solution)/shard_map/pallas_call | solution.py:605

commit v4 on v3

--- a/solution.py
+++ b/solution.py
@@ -16,7 +16,7 @@
 PARTS = 2
 PART = ROWS // PARTS
 WORDS = 7
-FAR = ((0, 0), (0, 1), (2, 0), (2, 1))
+FAR = ((0, 0), (2, 0), (0, 1), (2, 1))
 STEP = 32
 
 
@@ -133,14 +133,13 @@
 
         lax.fori_loop(0, n // STEP, body, 0)
 
-    def transposed(slot):
+    def transposed(slot, n):
         for j in range(4):
             cols = slice(j * 256, (j + 1) * 256)
-            v = hr[slot, :, cols].astype(F32).T.reshape(8, 2, 16, ROWS)
+            v = hr[slot, n * PART : (n + 1) * PART, cols].astype(F32).T.reshape(8, 2, 16, PART)
+            at_tokens = slice(slot * ROWS + n * PART, slot * ROWS + (n + 1) * PART)
             for cc in range(2):
-                ht[cc, j * 128 : (j + 1) * 128, slot * 256 : (slot + 1) * 256] = (
-                    v[:, cc].reshape(128, ROWS).astype(BF16)
-                )
+                ht[cc, j * 128 : (j + 1) * 128, at_tokens] = v[:, cc].reshape(128, PART).astype(BF16)
 
     loads[0].wait()
     pl.semaphore_wait(barrier, 1 + len(near_peers) + ends)
@@ -198,7 +197,8 @@
         forward(tu.at[1, 0], tu.at[1, 1], 0),
         forward(su.at[1, 0], su.at[1, 1], 1),
     ]
-    transposed(1)
+    for n in range(PARTS):
+        transposed(1, n)
     for cp in own_fwd:
         cp.wait_recv()
 
@@ -218,6 +218,12 @@
             1, dot_nt(su[1, 0], su[1, who]), dot_nt(tu[1, 0], tu[1, who])
         )
 
+    def own_gradient(nb, carry):
+        cols = pl.ds(pl.multiple_of(nb * 256, 256), 256)
+        early[nb] = dot_nn(e_near[:, 0:512], su[1, :, :, cols].reshape(512, 256))
+        return carry
+
+    lax.fori_loop(0, 4, own_gradient, 0)
     pass_on(2)
 
     s_fwd = []
@@ -227,9 +233,9 @@
             student_unit(slot, n * PART, PART)
             if n == PARTS - 1:
                 s_fwd.append(forward(su.at[slot, 0], su.at[slot, 1], 2 + slot // 2))
+            else:
+                transposed(slot, n)
             pass_on(3 + n * 2 + slot // 2)
-    for slot in (0, 2):
-        transposed(slot)
     for cp in s_fwd:
         cp.wait_recv()
     xs = 2 - 2 * c
@@ -240,7 +246,7 @@
         return rows, 2 - rows, jnp.where(f == 2, 1, 0)
 
     def near_student(j, carry):
-        ds[j] = dot_nt(su[1, 0], su[(j // 2) * 2, lax.rem(j, 2)])
+        ds[j] = dot_nt(su[1, 0], su[lax.rem(j, 2) * 2, j // 2])
         return carry
 
     lax.fori_loop(0, 4, near_student, 0)
@@ -252,11 +258,12 @@
 
     lax.fori_loop(0, 3, far_student, 0)
 
-    def near_part(j, n):
-        at_rows = pl.ds(pl.multiple_of(n * PART, PART), PART)
-        e_near[:, pl.ds(pl.multiple_of(512 + n * 4 * PART + j * PART, PART), PART)] = weigh(
-            1, ds[j, :, at_rows], dot_nt(tu[1, 0], tu[(j // 2) * 2, lax.rem(j, 2), at_rows])
-        )
+    def near_part(who, n):
+        rows = pl.ds(pl.multiple_of(n * PART, PART), PART)
+        cols = pl.ds(pl.multiple_of(512 + n * 4 * PART + who * 2 * PART, 2 * PART), 2 * PART)
+        student = jnp.concatenate([ds[2 * who, :, rows], ds[2 * who + 1, :, rows]], axis=1)
+        teacher = jnp.concatenate([tu[0, who, rows], tu[2, who, rows]], axis=0)
+        e_near[:, cols] = weigh(1, student, dot_nt(tu[1, 0], teacher))
 
     def near_rows(n, cols):
         return jnp.concatenate([su[slot, who, n * PART : (n + 1) * PART, cols] for slot, who in FAR], axis=0)
@@ -280,15 +287,7 @@
 
         copies = [arrived(0), arrived(2)]
 
-        def direct(j, cc):
-            near_part(2 * j, n)
-            return cc
-
-        def handed(j, cc):
-            near_part(2 * j + 1, n)
-            return cc
-
-        lax.fori_loop(0, 2, direct, 0)
+        near_part(0, n)
 
         @pl.when(n == PARTS - 1)
         def _():
@@ -296,18 +295,18 @@
 
         for cp in copies:
             cp.wait_recv()
-        lax.fori_loop(0, 2, handed, 0)
+        near_part(1, n)
 
         @pl.when(n == 0)
         def _():
             def block(nb, cc):
                 cols = pl.ds(pl.multiple_of(nb * 256, 256), 256)
-                early[nb] = dot_nn(e_near[:, 0:512], su[1, :, :, cols].reshape(512, 256)) + dot_nn(
-                    e_near[:, 512:1024], near_rows(0, cols)
-                )
+                early[nb] = early[nb] + dot_nn(e_near[:, 512:1024], near_rows(0, cols))
                 return cc
 
             lax.fori_loop(0, 4, block, 0)
+            for slot in (0, 2):
+                transposed(slot, PARTS - 1)
 
         return carry
 

time: 72.9 us -> 72 us (0.988)
  the two profiles are of different devices: /device:TPU:2 before, /device:TPU:32 now
where the time goes in v4:
time: 72 us; the launch traced here: 71.9 us
  Pallas kernels  71.2 us (99%)
    pallas_call x1, Pallas kernels, local(): pl.pallas_call(kernel, out_shape=results, in_specs=[anywhere] * 3, out_sp...  69.4 us
    pallas_call x1, Pallas kernels, local(): pl.pallas_call(handed_on, out_shape=results, in_specs=[pl.BlockSpec(memor...  1.88 us

profile of v4, /device:TPU:32, one launch (start us, length us, event | category | flops | bytes accessed | tf_op | source)
XLA Modules:
  0.0 71.9 jit_solution(11600628553541032749)
XLA Ops:
  0.6 69.4 %shard_map.50 = (bf16[256,1024]{1,0:T(8,128)(2,1)}, f32[16,1024]{1,0:T(8,128)}) custom-call(bf16[256,1024]{1,0:T(8,128)(2,1)} %bitcast.3, bf16[256,1024]{1,0:T(8,128)(2,1)} %bitcast.4, bf16[1024,1024]{1,0:T(8,128)(2,1)} %w_ref.1), custom_call_target="tpu_custom_call" | custom-call | tf_op jit(solution)/shard_map/pallas_call | solution.py:552
  70.0 1.9 %shard_map.51 = (bf16[256,1024]{1,0:T(8,128)(2,1)}, f32[16,1024]{1,0:T(8,128)}) custom-call(bf16[256,1024]{1,0:T(8,128)(2,1)} %get-tuple-element.6.hg_in, f32[16,1024]{1,0:T(8,128)} %get-tuple-element.7.wg_in), custom_call_target="tpu_custom_call" | custom-call | tf_op jit(solution)/shard_map/pallas_call | solution.py:604

commit v5 on v4

--- a/solution.py
+++ b/solution.py
@@ -16,6 +16,8 @@
 PARTS = 2
 PART = ROWS // PARTS
 WORDS = 7
+SUB = 64
+SUBS = ROWS // SUB
 FAR = ((0, 0), (2, 0), (0, 1), (2, 1))
 STEP = 32
 
@@ -152,10 +154,10 @@
         sems = (halo_s.at[i, n], halo_r.at[i, n], side[i])
         if isinstance(n, int) and n < PARTS:
             return remote(hr.at[1, part(n)], hr.at[slot, part(n)], *sems)
-        rows = pl.ds(pl.multiple_of((n - PARTS) * PART, PART), PART)
+        rows = pl.ds(pl.multiple_of((n - PARTS) * SUB, SUB), SUB)
         return remote(tu.at[1, 0, rows], tu.at[slot, 0, rows], *sems)
 
-    halo = [[halo_copy(i, n) for n in range(2 * PARTS)] for i in range(2)]
+    halo = [[halo_copy(i, n) for n in range(PARTS + SUBS)] for i in range(2)]
 
     def halo_send(n):
         for i in range(2):
@@ -179,7 +181,7 @@
     pass_on(0)
     loads[1].wait()
     teacher_unit()
-    for n in range(PARTS):
+    for n in range(SUBS):
         halo_send(PARTS + n)
     loads[2].wait()
     student_unit(1, 0, ROWS)
@@ -269,23 +271,23 @@
         return jnp.concatenate([su[slot, who, n * PART : (n + 1) * PART, cols] for slot, who in FAR], axis=0)
 
     def teacher_part(n, carry):
-        def arrived(slot):
+        def arrived(slot, m):
             i = slot // 2
-            rows = pl.ds(pl.multiple_of(n * PART, PART), PART)
+            rows = pl.ds(pl.multiple_of(m * SUB, SUB), SUB)
 
             @pl.when(has[i])
             def _():
-                halo_copy(1 - i, PARTS + n).wait_recv()
+                halo_copy(1 - i, PARTS + m).wait_recv()
 
             @pl.when(jnp.logical_not(has[i]))
             def _():
-                tu[slot, 0, rows] = jnp.zeros((PART, FEAT), BF16)
-
-            cp = teacher_forward(slot, n)
+                tu[slot, 0, rows] = jnp.zeros((SUB, FEAT), BF16)
+
+            cp = teacher_forward(slot, m)
             cp.start()
             return cp
 
-        copies = [arrived(0), arrived(2)]
+        copies = [arrived(slot, n * (SUBS // PARTS) + m) for m in range(SUBS // PARTS) for slot in (0, 2)]
 
         near_part(0, n)
 
@@ -311,7 +313,7 @@
         return carry
 
     def teacher_forward(slot, n):
-        rows = pl.ds(pl.multiple_of(n * PART, PART), PART)
+        rows = pl.ds(pl.multiple_of(n * SUB, SUB), SUB)
         m = 4 + n * 2 + slot // 2
         return remote(tu.at[slot, 0, rows], tu.at[slot, 1, rows], fwd_s.at[m], fwd_r.at[m], sib)
 
@@ -322,7 +324,7 @@
 
     lax.fori_loop(0, PARTS, teacher_part, 0)
     far_weight(2, 0)
-    for n in range(PARTS):
+    for n in range(SUBS):
         for slot in (0, 2):
             fwd.append(teacher_forward(slot, n))
 
@@ -586,8 +588,8 @@
             vm((ROWS, FEAT), BF16),
             vm((ROWS, FEAT), BF16),
             dma((3,)), dma((1,)),
-            dma((2, 2 * PARTS)), dma((2, 2 * PARTS)),
-            dma((4 + 2 * PARTS,)), dma((4 + 2 * PARTS,)),
+            dma((2, PARTS + SUBS)), dma((2, PARTS + SUBS)),
+            dma((4 + 2 * SUBS,)), dma((4 + 2 * SUBS,)),
             dma((2, 4)), dma((2, 4)),
             dma((4,)), dma((4,)),
             dma((3,)), dma((3,)),

time: 72 us -> 72.2 us (level)
  no operation moved by 1% of the time
where the time goes in v5:
time: 72.2 us; the launch traced here: 72.1 us
  Pallas kernels  71.4 us (99%)
    pallas_call x1, Pallas kernels, local(): pl.pallas_call(kernel, out_shape=results, in_specs=[anywhere] * 3, out_sp...  69.5 us
    pallas_call x1, Pallas kernels, local(): pl.pallas_call(handed_on, out_shape=results, in_specs=[pl.BlockSpec(memor...  1.88 us

profile of v5, /device:TPU:32, one launch (start us, length us, event | category | flops | bytes accessed | tf_op | source)
XLA Modules:
  0.0 72.1 jit_solution(8428025829080640421)
XLA Ops:
  0.6 69.5 %shard_map.50 = (bf16[256,1024]{1,0:T(8,128)(2,1)}, f32[16,1024]{1,0:T(8,128)}) custom-call(bf16[256,1024]{1,0:T(8,128)(2,1)} %bitcast.3, bf16[256,1024]{1,0:T(8,128)(2,1)} %bitcast.4, bf16[1024,1024]{1,0:T(8,128)(2,1)} %w_ref.1), custom_call_target="tpu_custom_call" | custom-call | tf_op jit(solution)/shard_map/pallas_call | solution.py:554
  70.2 1.9 %shard_map.51 = (bf16[256,1024]{1,0:T(8,128)(2,1)}, f32[16,1024]{1,0:T(8,128)}) custom-call(bf16[256,1024]{1,0:T(8,128)(2,1)} %get-tuple-element.6.hg_in, f32[16,1024]{1,0:T(8,128)} %get-tuple-element.7.wg_in), custom_call_target="tpu_custom_call" | custom-call | tf_op jit(solution)/shard_map/pallas_call | solution.py:606
